TPU v7x, 1024 devices: a whole 8x8x8 slice. The times are simulated.
1024 devices in a mesh: box: 64 (over y_lo, z, core), dir: 16 (over x, y_hi).
Axes of the slice: x: 8, y: 8 (y_hi: 2, y_lo: 4; y = y_hi * 4 + y_lo), z: 8, core: 2. Of those that a mesh axis runs over, the one named last changes fastest.
Arguments:
- child_out: bfloat16 [8192, 8, 512], P('box', None, 'dir'), may hold values from -6 to 6
- interp: bfloat16 [512, 2048], replicated, may hold values from -0.25 to 0.25
- shift_angle: float32 [8, 2048], replicated, may hold values from -3.140625 to 3.140625
- translators: float32 [343, 2, 2048], P(None, None, 'dir'), may hold values from -3 to 3
- nbr_index: int32 [1024, 27], replicated, may hold values from 0 to 1023, as said below
- nbr_trans: int32 [1024, 27], replicated, may hold values from 0 to 342, as said below
Outputs:
- child_in: bfloat16 [8192, 8, 512], P('box', None, 'dir')
Inputs may be any that keep to these rules, and one draw needn't show every extreme that they name: Parents lie on a periodic slab indexed in Morton order: all index bits but the top two are taken in turn by the first two coordinates (lowest bit first), and the top two bits give the third coordinate, which thus runs over 4 layers. Row p holds 27 distinct offsets of largest component 2 or 3, and nbr_index[p, n] is the parent at that offset from p, coordinates taken periodically. nbr_trans[p, n] = (dx + 3) * 49 + (dy + 3) * 7 + (dz + 3) for the offset (dx, dy, dz) of nbr_index[p, n].
All inputs are finite; a program needn't handle non-finite values.
Results may differ from a plain program's by a relative error of at most 0.012.
Values may be sent and summed in bfloat16 or wider, within the bound.
A program may use at most 32 MiB of HBM per device.

v0:
```python
import jax
import jax.numpy as jnp
from jax import lax
from jax.sharding import Mesh
from jax.sharding import PartitionSpec as P

CH = 8
DIR = ("dir_0", "dir_1")


anterp_scale = 0.125


def sum_by_axis(shard, axes, dim):
    if not axes:
        return shard
    nearer = lax.psum_scatter(shard, axes[0], scatter_dimension=dim, tiled=True)
    return sum_by_axis(nearer, axes[1:], dim)


def cmul(field, real_part, imag_part):
    half = field.shape[-2] // 2
    left = field[..., :half, :]
    right = field[..., half:, :]
    return jnp.concatenate(
        [left * real_part - right * imag_part, left * imag_part + right * real_part], axis=-2
    )


def phases(count, table):
    octants = jnp.arange(count, dtype=jnp.int32) % table.shape[0]
    onehot = (octants[:, None] == jnp.arange(table.shape[0], dtype=jnp.int32)[None, :]).astype(
        jnp.float32
    )
    return jnp.dot(onehot, table, precision=lax.Precision.HIGHEST)


def translate(source, partners, offsets, table):

    def add_slot(slot, total):
        which = lax.dynamic_index_in_dim(partners, slot, 1, keepdims=False)
        offset_col = lax.dynamic_index_in_dim(offsets, slot, 1, keepdims=False)
        picked = jnp.take(source, which, axis=0).astype(jnp.float32)
        factors = jnp.take(table, offset_col, axis=0)
        return total + cmul(picked, factors[:, 0:1, :], factors[:, 1:2, :])

    empty = jnp.zeros((partners.shape[0], source.shape[1], source.shape[2]), jnp.float32)
    total = lax.fori_loop(0, partners.shape[1], add_slot, empty)
    return total.astype(jnp.bfloat16)


def per_device(child_out, interp, shift_angle, translators, nbr_index, nbr_trans):
    cols = child_out.shape[1]
    child_cnt = child_out.shape[0]
    par_cnt = child_cnt // CH
    npd = interp.shape[1]
    ndir = lax.axis_size(DIR)
    dir_at = lax.axis_index(DIR)
    box_at = lax.axis_index("box")
    pdir = npd // ndir
    cos_table = jnp.cos(shift_angle)
    sin_table = jnp.sin(shift_angle)
    my_cols = lax.dynamic_slice_in_dim(interp, dir_at * pdir, pdir, 1)
    cos_mine = phases(child_cnt, lax.dynamic_slice_in_dim(cos_table, dir_at * pdir, pdir, 1))[
        :, None, :
    ]
    sin_mine = phases(child_cnt, lax.dynamic_slice_in_dim(sin_table, dir_at * pdir, pdir, 1))[
        :, None, :
    ]
    interp_child = jnp.einsum(
        "bck,kj->bcj",
        lax.all_gather(child_out, DIR, axis=2, tiled=True),
        my_cols,
        preferred_element_type=jnp.float32,
    )
    parent_out = (
        cmul(interp_child, cos_mine, sin_mine)
        .reshape(par_cnt, CH, cols, pdir)
        .sum(axis=1)
        .astype(jnp.bfloat16)
    )
    everyone = lax.all_gather(parent_out, "box", axis=0, tiled=True)
    partners = lax.dynamic_slice_in_dim(nbr_index, box_at * par_cnt, par_cnt, 0)
    offsets = lax.dynamic_slice_in_dim(nbr_trans, box_at * par_cnt, par_cnt, 0)
    parent_in = translate(everyone, partners, offsets, translators)
    down = (
        jnp.broadcast_to(parent_in[:, None], (par_cnt, CH, cols, pdir))
        .reshape(child_cnt, cols, pdir)
        .astype(jnp.float32)
    )
    back = cmul(down, cos_mine, -sin_mine).astype(jnp.bfloat16)
    terms = anterp_scale * jnp.einsum(
        "bcj,kj->bck", back, my_cols, preferred_element_type=jnp.float32
    )
    child_in = sum_by_axis(terms, DIR, 2).astype(jnp.bfloat16)
    return child_in


def solution(mesh):
    split = Mesh(mesh.devices.reshape(mesh.shape["box"], 8, 2), ("box", "dir_0", "dir_1"))
    in_specs = (P("box", None, DIR), P(), P(), P(None, None, DIR), P(), P())
    out_specs = P("box", None, DIR)
    return jax.shard_map(
        per_device, mesh=split, in_specs=in_specs, out_specs=out_specs, check_vma=False
    )
```

profile of v0, /device:TPU:1, one launch (start us, length us, event | category | flops | bytes accessed | tf_op | source)
XLA Modules:
  0.0 438.0 jit_solution(7315590184894268633)
XLA Ops:
  7.3 0.9 fusion.9
  8.2 0.9 fusion.22
  9.2 105.0 %all-gather.3.cloned.1.call-done = bf16[128,8,512]{0,2,1:T(8,128)(2,1)} async-done(((bf16[128,8,32]{0,2,1:T(8,128)(2,1)}), bf16[128,8,512]{0,2,1:T(8,128)(2,1)}) %all-gather.3.cloned.1.call-update) | async-done | bytes 1048592 | tf_op jit(solution)/shard_map/all_gather | solution.py:72
  114.1 1.8 convolution_bitcast_fusion
  117.7 122.3 %all-gather.5.cloned.1.call-done = bf16[1024,8,128]{2,1,0:T(8,128)(2,1)} async-done(((bf16[16,8,128]{2,1,0:T(8,128)(2,1)}), bf16[1024,8,128]{2,1,0:T(8,128)(2,1)}) %all-gather.5.cloned.1.call-update) | async-done | bytes 2097168 | tf_op jit(solution)/shard_map/all_gather | solution.py:82
  240.0 110.0 %while.14 = (s32[]{:T(128)}, f32[16,8,128]{2,1,0:T(8,128)S(1)}, s32[16,27]{0,1:T(8,128)S(1)}, bf16[1024,8,128]{2,1,0:T(8,128)(2,1)}, s32[16,27]{0,1:T(8,128)S(1)...) while((s32[]{:T(128)}, f32[16,8,128]{2,1,0:T(8,128)S(1)}, s32[16,27]{0,1:T(8,128)S(1)}, ...), condition=%wide.region_2.3_spmd.clone, body=%wide.region_1.2_spmd.clone.sunk | while | flops 137411 | bytes 615075 | solution.py:48
  240.0 1.6 gather_fusion.1
  241.7 2.2 gather_fusion
  244.1 1.6 gather_fusion.1
  245.8 2.2 gather_fusion
  248.2 1.6 gather_fusion.1
  249.8 2.2 gather_fusion
  252.2 1.6 gather_fusion.1
  253.9 2.2 gather_fusion
  256.3 1.6 gather_fusion.1
  258.0 2.2 gather_fusion
  260.4 1.6 gather_fusion.1
  262.1 2.2 gather_fusion
  264.5 1.6 gather_fusion.1
  266.2 2.2 gather_fusion
  268.5 1.6 gather_fusion.1
  270.2 2.2 gather_fusion
  272.6 1.6 gather_fusion.1
  274.3 2.2 gather_fusion
  276.7 1.6 gather_fusion.1
  278.4 2.2 gather_fusion
  280.8 1.6 gather_fusion.1
  282.5 2.2 gather_fusion
  284.8 1.6 gather_fusion.1
  286.5 2.2 gather_fusion
  288.9 1.6 gather_fusion.1
  290.6 2.2 gather_fusion
  293.0 1.6 gather_fusion.1
  294.7 2.2 gather_fusion
  297.1 1.6 gather_fusion.1
  298.8 2.2 gather_fusion
  301.1 1.6 gather_fusion.1
  302.8 2.2 gather_fusion
  305.2 1.6 gather_fusion.1
  306.9 2.2 gather_fusion
  309.3 1.6 gather_fusion.1
  311.0 2.2 gather_fusion
  313.4 1.6 gather_fusion.1
  315.1 2.2 gather_fusion
  317.4 1.6 gather_fusion.1
  319.1 2.2 gather_fusion
  321.5 1.6 gather_fusion.1
  323.2 2.2 gather_fusion
  325.6 1.6 gather_fusion.1
  327.3 2.2 gather_fusion
  329.7 1.6 gather_fusion.1
  331.4 2.2 gather_fusion
  333.7 1.6 gather_fusion.1
  335.4 2.2 gather_fusion
  337.8 1.6 gather_fusion.1
  339.5 2.2 gather_fusion
  341.9 1.6 gather_fusion.1
  343.6 2.2 gather_fusion
  346.0 1.6 gather_fusion.1
  347.7 2.2 gather_fusion
  350.2 1.8 convolution_multiply_fusion
  352.0 42.1 %reduce-scatter.3.cloned.1.call-done = f32[128,8,64]{0,2,1:T(8,128)} async-done(((f32[128,8,512]{0,2,1:T(8,128)}), f32[128,8,64]{0,2,1:T(8,128)}) %reduce-scatter.3.cloned.1.call-update) | async-done | bytes 262160 | tf_op jit(solution)/shard_map/reduce_scatter | solution.py:17
  394.1 35.8 %reduce-scatter.5.cloned.1.call-done = f32[128,8,32]{0,2,1:T(8,128)} async-done(((f32[128,8,64]{0,2,1:T(8,128)}), f32[128,8,32]{0,2,1:T(8,128)}) %reduce-scatter.5.cloned.1.call-update) | async-done | bytes 131088 | tf_op jit(solution)/shard_map/reduce_scatter | solution.py:17
  430.0 1.5 convert_element_type.30
  (236 shorter events, 9.7 us)
Async XLA Ops:
  6.5 107.6 %copy-start = (bf16[512,2048]{1,0:T(8,128)(2,1)S(1)}, bf16[512,2048]{1,0:T(8,128)(2,1)}, u32[]{:S(2)}) copy-start(bf16[512,2048]{1,0:T(8,128)(2,1)} %param.9) | copy-start | bytes 6291460
  6.5 107.6 %all-gather.3.cloned.1.call-start = ((), (), s32[]{:S(2)}) async-start(), calls=%async_computation.2 | async-start | bytes 1114112 | tf_op jit(solution)/shard_map/all_gather | solution.py:72
  7.3 232.7 %all-gather.5.cloned.1.call-start = ((), (), s32[]{:S(2)}) async-start(), calls=%async_computation.3 | async-start | bytes 2129920 | tf_op jit(solution)/shard_map/all_gather | solution.py:82
  116.8 277.3 %reduce-scatter.3.cloned.1.call-start = ((), (), s32[]{:S(2)}) async-start(), calls=%async_computation.4 | async-start | bytes 2359296 | tf_op jit(solution)/shard_map/reduce_scatter | solution.py:17
  352.0 78.0 %reduce-scatter.5.cloned.1.call-start = ((), (), s32[]{:S(2)}) async-start(), calls=%async_computation.5 | async-start | bytes 393216 | tf_op jit(solution)/shard_map/reduce_scatter | solution.py:17
Sparse Core Ops, SparseCore 0:
  11.6 102.5 all-gather.2
  116.9 123.0 all-gather.4
  352.1 41.9 reduce-scatter.2
  397.3 32.5 reduce-scatter.4
where the time goes:
time: 440 us; the launch traced here: 438 us
  waiting for transfers between devices  306 us (70%)
  local copies, waits for them, and re-layouts  103 us (23%)
  between operations  13.2 us (3%)
  other arithmetic  8.42 us (2%)
  matrix products  5.39 us (1%)
    all_gather x1, waiting for transfers between devices, per_device(): everyone = lax.all_gather(parent_out, 'box', axis=0, tiled=True)  122 us
    all_gather x1, waiting for transfers between devices, per_device(): lax.all_gather(child_out, DIR, axis=2, tiled=True)  105 us
    reduce_scatter x2, waiting for transfers between devices, sum_by_axis(): nearer = lax.psum_scatter(shard, axes[0], scatter_dimension=dim, tiled=True)  77.9 us
    gather x27, local copies, waits for them, and re-layouts, add_slot(): picked = jnp.take(source, which, axis=0).astype(jnp.float32)  58.5 us
    gather x27, local copies, waits for them, and re-layouts, add_slot(): factors = jnp.take(table, offset_col, axis=0)  42.4 us
  transfers between devices with their start and end apart: 4, of which 4 were waited for; matrix products, arithmetic and copies ran while one was open for 1% of the time, Pallas kernels for 0%

commit v1 on v0

v1 whole, which is shorter than its diff:
```python
import jax
import jax.numpy as jnp
from jax import lax
from jax.experimental import pallas as pl
from jax.experimental.pallas import tpu as pltpu
from jax.sharding import PartitionSpec as P

MESH = pl.DeviceIdType.MESH
F32 = jnp.float32
BF16 = jnp.bfloat16

NCD = 512
NPD = 2048
NBR = 27
NT = 343
NDIR = 16
RHS = 4
LAYERS = 4
BLK = 16
LANES = 128
GROUP = LAYERS * BLK
EDGE = 48
HALO = GROUP + 8 * EDGE
HALO_PAD = 512
NT_PAD = 384
STEP = 9
TURNS = [m for m in range(9) if m != 4]


def swap_lane_blocks(tiles):
    lane = lax.broadcasted_iota(jnp.int32, tiles[0].shape, 1)
    low = (lane // 32) % 2 == 0
    mid = (lane // 64) % 2 == 0
    v0, v1, v2, v3 = tiles

    def pair(a, b, keep, width):
        first = jnp.where(keep, a, pltpu.roll(b, width, 1))
        second = jnp.where(keep, pltpu.roll(a, LANES - width, 1), b)
        return first, second

    v0, v1 = pair(v0, v1, low, 32)
    v2, v3 = pair(v2, v3, low, 32)
    v0, v2 = pair(v0, v2, mid, 64)
    v1, v3 = pair(v1, v3, mid, 64)
    return [v0, v1, v2, v3]


def kernel(
    child_hbm, interp_hbm, angle_hbm, trans_hbm, nidx_hbm, ntr_hbm, out_ref,
    child_v, interp_v, angle_v, trans_v, nidx_v, ntr_v,
    send_a, recv_a, lhs_v, cos_v, sin_v, send_p, recv_p, field_v, turned_v,
    pick_v, factor_v, table_hi, table_lo, send_q, recv_q, back_v, send_c, recv_c,
    load_sem, send_sem, recv_sem,
):
    box = lax.axis_index("box")
    me = lax.axis_index("dir")
    layer = box // 16
    zc = box % 16
    xb = zc % 2 + 2 * ((zc // 4) % 2)
    yb = (zc // 2) % 2 + 2 * (zc // 8)

    loads = [
        pltpu.make_async_copy(src, dst, load_sem.at[i])
        for i, (src, dst) in enumerate(
            [
                (child_hbm, child_v),
                (angle_hbm, angle_v),
                (nidx_hbm, nidx_v),
                (ntr_hbm, ntr_v),
                (interp_hbm, interp_v),
                (trans_hbm, trans_v),
            ]
        )
    ]
    for load in loads:
        load.start()

    def plane(t):
        return (layer + t // NDIR) % LAYERS, (me + t) % NDIR

    def neighbour(m):
        dx, dy = m % 3 - 1, m // 3 - 1
        tx, ty = (xb - dx + 4) % 4, (yb - dy + 4) % 4
        return layer * 16 + tx % 2 + 2 * (ty % 2) + 4 * (tx // 2) + 8 * (ty // 2)

    barrier = pltpu.get_barrier_semaphore()

    def greet(t, carry):
        to_layer, to_dir = plane(t)
        pl.semaphore_signal(
            barrier, inc=1, device_id=(to_layer * 16 + zc, to_dir), device_id_type=MESH
        )
        return carry

    lax.fori_loop(1, LAYERS * NDIR, greet, 0)
    for m in TURNS:
        pl.semaphore_signal(barrier, inc=1, device_id=(neighbour(m), me), device_id_type=MESH)

    loads[0].wait()
    halves = []
    for h in range(2):
        block = child_v[h * LANES : (h + 1) * LANES, :].astype(F32)
        halves.append(block.T.reshape(NDIR, 8, LANES))
    send_a[...] = jnp.concatenate(halves, axis=1).astype(BF16)

    pl.semaphore_wait(barrier, LAYERS * NDIR - 1 + len(TURNS))

    def send_child(t, carry):
        to = (me + t) % NDIR
        pltpu.make_async_remote_copy(
            src_ref=send_a.at[to], dst_ref=recv_a.at[me],
            send_sem=send_sem.at[0], recv_sem=recv_sem.at[0],
            device_id=(box, to), device_id_type=MESH,
        ).start()
        return carry

    lax.fori_loop(1, NDIR, send_child, 0)
    recv_a[me] = send_a[me]

    loads[1].wait()
    cos_v[...] = jnp.cos(angle_v[...])
    sin_v[...] = jnp.sin(angle_v[...])

    loads[2].wait()
    loads[3].wait()
    lane = lax.broadcasted_iota(jnp.int32, (32, LANES), 1)

    def mine(ref):
        parts = jnp.zeros((32, LANES), jnp.int32)
        for q in range(LAYERS):
            at = pl.multiple_of(q * 256 + (zc // 8) * LANES, LANES)
            cols = jnp.concatenate(
                [ref[:, pl.ds(at, LANES)], jnp.zeros((32 - NBR, LANES), jnp.int32)], axis=0
            )
            cols = pltpu.roll(cols, (q * BLK - (zc % 8) * BLK + LANES) % LANES, 1)
            parts = jnp.where(lane // BLK == q, cols, parts)
        return parts

    source = mine(nidx_v)
    sx = source % 2 + 2 * ((source // 4) % 2) + 4 * ((source // 16) % 2) + 8 * ((source // 64) % 2)
    sy = (source // 2) % 2 + 2 * ((source // 8) % 2) + 4 * ((source // 32) % 2) + 8 * ((source // 128) % 2)
    sl = source // 256
    u = (sx - 4 * xb + 20) % 16
    v = (sy - 4 * yb + 20) % 16
    bx, x, by, y = u // 4, u % 4, v // 4, v % 4
    turn = by * 3 + bx
    base = GROUP + EDGE * (turn - (turn > 4).astype(jnp.int32))
    by_y = base + 16 * (y - (by == 0).astype(jnp.int32)) + 4 * x + sl
    by_x = base + 16 * (x - (bx == 0).astype(jnp.int32)) + 4 * y + sl
    row = jnp.where(by != 1, by_y, jnp.where(bx != 1, by_x, 16 * y + 4 * x + sl))
    source_rows = row.astype(F32).T[0:GROUP, :]
    factor_rows = mine(ntr_v).astype(F32).T[0:GROUP, :]

    slot_no = lax.broadcasted_iota(jnp.int32, (GROUP, HALO_PAD), 1).astype(F32)
    for n in range(NBR):
        pick_v[n * GROUP : (n + 1) * GROUP, :] = jnp.where(
            source_rows[:, n : n + 1] == slot_no, 1.0, 0.0
        ).astype(BF16)

    loads[4].wait()
    pltpu.make_async_copy(
        recv_a.at[pl.ds(0, NDIR - 1)], recv_a.at[pl.ds(0, NDIR - 1)], recv_sem.at[0]
    ).wait()
    for g in range(4):
        tiles = swap_lane_blocks([recv_a[4 * g + i].astype(F32) for i in range(4)])
        for c in range(4):
            lhs_v[c * 16 : (c + 1) * 16, g * LANES : (g + 1) * LANES] = tiles[c].astype(BF16)
    for d2 in range(NDIR // 2):
        prod = jnp.dot(
            lhs_v[...], interp_v[:, d2 * 256 : (d2 + 1) * 256], preferred_element_type=F32
        )
        for i in range(2):
            d = d2 * 2 + i
            cosine = cos_v[:, d * LANES : (d + 1) * LANES]
            sine = sin_v[:, d * LANES : (d + 1) * LANES]
            for c in range(RHS):
                re = prod[c * 16 : c * 16 + 8, i * LANES : (i + 1) * LANES]
                im = prod[c * 16 + 8 : c * 16 + 16, i * LANES : (i + 1) * LANES]
                out_re = jnp.sum(re * cosine - im * sine, axis=0, keepdims=True)
                out_im = jnp.sum(re * sine + im * cosine, axis=0, keepdims=True)
                send_p[d * RHS + c, 0:1, :] = out_re.astype(BF16).astype(F32)
                send_p[d * RHS + c, 1:2, :] = out_im.astype(BF16).astype(F32)

    my_row = 16 * ((me // 2) % 2 + 2 * (me // 8)) + 4 * (me % 2 + 2 * ((me // 4) % 2)) + layer

    def send_parent(t, carry):
        to_layer, to_dir = plane(t)
        pltpu.make_async_remote_copy(
            src_ref=send_p.at[to_dir * RHS + to_layer], dst_ref=recv_p.at[my_row],
            send_sem=send_sem.at[1], recv_sem=recv_sem.at[1],
            device_id=(to_layer * 16 + zc, to_dir), device_id_type=MESH,
        ).start()
        return carry

    lax.fori_loop(1, LAYERS * NDIR, send_parent, 0)
    recv_p[my_row] = send_p[me * RHS + layer]

    loads[5].wait()
    for h in range(2):
        values = trans_v[:, h, :]
        hi = values.astype(BF16)
        lo = (values - hi.astype(F32)).astype(BF16)
        pad = jnp.zeros((NT_PAD - NT, LANES), BF16)
        table_hi[:, h * LANES : (h + 1) * LANES] = jnp.concatenate([hi, pad], axis=0)
        table_lo[:, h * LANES : (h + 1) * LANES] = jnp.concatenate([lo, pad], axis=0)
    field_v[HALO:HALO_PAD, :] = jnp.zeros((HALO_PAD - HALO, 2 * LANES), BF16)

    pltpu.make_async_copy(
        recv_p.at[pl.ds(0, GROUP - 1)], recv_p.at[pl.ds(0, GROUP - 1)], recv_sem.at[1]
    ).wait()
    for h in range(2):
        cols = slice(h * LANES, (h + 1) * LANES)
        field_v[0:GROUP, cols] = recv_p[:, h, :].astype(BF16)
        turned_v[:, cols] = jnp.concatenate(
            [recv_p[16 * gy + 4 * gx : 16 * gy + 4 * gx + 4, h, :] for gx in range(4) for gy in range(4)],
            axis=0,
        ).astype(BF16)

    for k, m in enumerate(TURNS):
        dx, dy = m % 3 - 1, m // 3 - 1
        first = 16 if (dy if dy else dx) < 0 else 0
        pltpu.make_async_remote_copy(
            src_ref=(field_v if dy else turned_v).at[pl.ds(first, EDGE)],
            dst_ref=field_v.at[pl.ds(GROUP + EDGE * k, EDGE)],
            send_sem=send_sem.at[2], recv_sem=recv_sem.at[2],
            device_id=(neighbour(m), me), device_id_type=MESH,
        ).start()

    factor_no = lax.broadcasted_iota(jnp.int32, (GROUP, NT_PAD), 1).astype(F32)
    for s in range(0, NBR, STEP):
        chosen = jnp.concatenate(
            [
                jnp.where(factor_rows[:, n : n + 1] == factor_no, 1.0, 0.0).astype(BF16)
                for n in range(s, s + STEP)
            ],
            axis=0,
        )
        factor_v[s * GROUP : (s + STEP) * GROUP, :] = jnp.dot(
            chosen, table_hi[...], preferred_element_type=F32
        ) + jnp.dot(chosen, table_lo[...], preferred_element_type=F32)

    arrived = field_v.at[pl.ds(GROUP, 8 * EDGE)]
    pltpu.make_async_copy(arrived, arrived, recv_sem.at[2]).wait()
    sum_re = jnp.zeros((GROUP, LANES), F32)
    sum_im = jnp.zeros((GROUP, LANES), F32)
    for s in range(0, NBR, STEP):
        picked = jnp.dot(
            pick_v[s * GROUP : (s + STEP) * GROUP, :], field_v[...], preferred_element_type=F32
        )
        for n in range(STEP):
            re = picked[n * GROUP : (n + 1) * GROUP, 0:LANES]
            im = picked[n * GROUP : (n + 1) * GROUP, LANES : 2 * LANES]
            at = (s + n) * GROUP
            t_re = factor_v[at : at + GROUP, 0:LANES]
            t_im = factor_v[at : at + GROUP, LANES : 2 * LANES]
            sum_re = sum_re + (re * t_re - im * t_im)
            sum_im = sum_im + (re * t_im + im * t_re)
    send_q[:, 0, :] = sum_re.astype(BF16).astype(F32)
    send_q[:, 1, :] = sum_im.astype(BF16).astype(F32)

    def send_sum(t, carry):
        to_layer, to_dir = plane(t)
        pltpu.make_async_remote_copy(
            src_ref=send_q.at[to_layer * BLK + to_dir], dst_ref=recv_q.at[me * RHS + layer],
            send_sem=send_sem.at[3], recv_sem=recv_sem.at[3],
            device_id=(to_layer * 16 + zc, to_dir), device_id_type=MESH,
        ).start()
        return carry

    lax.fori_loop(1, LAYERS * NDIR, send_sum, 0)
    recv_q[me * RHS + layer] = send_q[layer * BLK + me]

    pltpu.make_async_copy(
        recv_q.at[pl.ds(0, GROUP - 1)], recv_q.at[pl.ds(0, GROUP - 1)], recv_sem.at[3]
    ).wait()
    for d in range(NDIR):
        cosine = cos_v[:, d * LANES : (d + 1) * LANES]
        sine = sin_v[:, d * LANES : (d + 1) * LANES]
        for c in range(RHS):
            re = recv_q[d * RHS + c, 0:1, :]
            im = recv_q[d * RHS + c, 1:2, :]
            back_v[c * 16 : (c + 1) * 16, d * LANES : (d + 1) * LANES] = jnp.concatenate(
                [re * cosine + im * sine, im * cosine - re * sine], axis=0
            ).astype(BF16)
    prod = 0.125 * lax.dot_general(
        back_v[...], interp_v[...], (((1,), (1,)), ((), ())), preferred_element_type=F32
    )
    for g in range(4):
        tiles = swap_lane_blocks(
            [prod[c * 16 : (c + 1) * 16, g * LANES : (g + 1) * LANES] for c in range(4)]
        )
        for i in range(4):
            send_c[4 * g + i] = tiles[i].astype(BF16)

    def send_result(t, carry):
        to = (me + t) % NDIR
        pltpu.make_async_remote_copy(
            src_ref=send_c.at[to], dst_ref=recv_c.at[me],
            send_sem=send_sem.at[4], recv_sem=recv_sem.at[4],
            device_id=(box, to), device_id_type=MESH,
        ).start()
        return carry

    lax.fori_loop(1, NDIR, send_result, 0)
    recv_c[me] = send_c[me]
    pltpu.make_async_copy(
        recv_c.at[pl.ds(0, NDIR - 1)], recv_c.at[pl.ds(0, NDIR - 1)], recv_sem.at[4]
    ).wait()
    result = recv_c[...].astype(F32)
    for h in range(2):
        block = result[:, h * 8 : (h + 1) * 8, :].reshape(LANES, LANES)
        out_ref[h * LANES : (h + 1) * LANES, :] = block.T.astype(BF16)

    sent = [
        send_a.at[pl.ds(0, NDIR - 1)],
        send_p.at[pl.ds(0, GROUP - 1)],
        field_v.at[pl.ds(0, 8 * EDGE)],
        send_q.at[pl.ds(0, GROUP - 1)],
        send_c.at[pl.ds(0, NDIR - 1)],
    ]
    for i, ref in enumerate(sent):
        pltpu.make_async_copy(ref, ref, send_sem.at[i]).wait()


def per_device(child_out, interp, shift_angle, translators, nbr_index, nbr_trans):
    count, cols, width = child_out.shape
    children = child_out.transpose(1, 2, 0).reshape(cols * width, count)
    out = pl.pallas_call(
        kernel,
        out_shape=jax.ShapeDtypeStruct((cols * width, count), BF16),
        in_specs=[pl.BlockSpec(memory_space=pl.ANY)] * 6,
        out_specs=pl.BlockSpec(memory_space=pltpu.VMEM),
        scratch_shapes=[
            pltpu.VMEM((cols * width, count), BF16),
            pltpu.VMEM((NCD, NPD), BF16),
            pltpu.VMEM((8, NPD), F32),
            pltpu.VMEM((NT, 2, LANES), F32),
            pltpu.VMEM((NBR, 1024), jnp.int32),
            pltpu.VMEM((NBR, 1024), jnp.int32),
            pltpu.VMEM((NDIR, 16, LANES), BF16),
            pltpu.VMEM((NDIR, 16, LANES), BF16),
            pltpu.VMEM((64, NCD), BF16),
            pltpu.VMEM((8, NPD), F32),
            pltpu.VMEM((8, NPD), F32),
            pltpu.VMEM((GROUP, 2, LANES), F32),
            pltpu.VMEM((GROUP, 2, LANES), F32),
            pltpu.VMEM((HALO_PAD, 2 * LANES), BF16),
            pltpu.VMEM((GROUP, 2 * LANES), BF16),
            pltpu.VMEM((NBR * GROUP, HALO_PAD), BF16),
            pltpu.VMEM((NBR * GROUP, 2 * LANES), F32),
            pltpu.VMEM((NT_PAD, 2 * LANES), BF16),
            pltpu.VMEM((NT_PAD, 2 * LANES), BF16),
            pltpu.VMEM((GROUP, 2, LANES), F32),
            pltpu.VMEM((GROUP, 2, LANES), F32),
            pltpu.VMEM((64, NPD), BF16),
            pltpu.VMEM((NDIR, 16, LANES), BF16),
            pltpu.VMEM((NDIR, 16, LANES), BF16),
            pltpu.SemaphoreType.DMA((6,)),
            pltpu.SemaphoreType.DMA((5,)),
            pltpu.SemaphoreType.DMA((5,)),
        ],
        compiler_params=pltpu.CompilerParams(
            collective_id=0, has_side_effects=True, vmem_limit_bytes=40 * 1024 * 1024
        ),
    )(children, interp, shift_angle, translators, nbr_index.T, nbr_trans.T)
    return out.reshape(cols, width, count).transpose(2, 0, 1)


def solution(mesh):
    return jax.shard_map(
        per_device,
        mesh=mesh,
        in_specs=(P("box", None, "dir"), P(), P(), P(None, None, "dir"), P(), P()),
        out_specs=P("box", None, "dir"),
        check_vma=False,
    )
```

time: 440 us -> 70.4 us (0.16)
  waiting for transfers between devices: 306 us -> 0 us
  local copies, waits for them, and re-layouts: 103 us -> 6.69 us
  Pallas kernels: 0 us -> 63.3 us
  between operations: 13.2 us -> 0.02 us
  other arithmetic: 8.42 us -> 0 us
  matrix products: 5.39 us -> 0 us
    all_gather x2 -> x0, waiting for transfers between devices: 227 us -> none  [the longest x1 122 us: per_device(): everyone = lax.all_gather(parent_out, 'box', axis=0, tiled=True)]
    gather x54 -> x0, local copies, waits for them, and re-layouts: 101 us -> none  [the longest x27 58.5 us: add_slot(): picked = jnp.take(source, which, axis=0).astype(jnp.float32)]
    reduce_scatter x2 -> x0, waiting for transfers between devices: 77.9 us -> none  [sum_by_axis(): nearer = lax.psum_scatter(shard, axes[0], scatter_dimension=dim, tiled=True)]
    pallas_call x0 -> x1, Pallas kernels: none -> 63.3 us  [per_device(): pl.pallas_call(kernel, out_shape=jax.ShapeDtypeStruct((cols * width, coun...]
    unnamed x2 -> x13, local copies, waits for them, and re-layouts: 0.01 us -> 6.69 us
    dot_general x4 -> x0, matrix products: 5.39 us -> none  [the longest x2 1.84 us: phases(): return jnp.dot(onehot, table, precision=lax.Precision.HIGHEST)]
  transfers between devices with their start and end apart: 4 -> 0, of which waited for: 4 -> 0; matrix products, arithmetic and copies ran while one was open for 1% -> 0% of each run, Pallas kernels for 0% -> 0%
where the time goes in v1:
time: 70.4 us; the launch traced here: 70 us
  Pallas kernels  63.3 us (90%)
  local copies, waits for them, and re-layouts  6.69 us (10%)
    pallas_call x1, Pallas kernels, per_device(): pl.pallas_call(kernel, out_shape=jax.ShapeDtypeStruct((cols * width, coun...  63.3 us
    unnamed x13, local copies, waits for them, and re-layouts  6.69 us

profile of v1, /device:TPU:1, one launch (start us, length us, event | category | flops | bytes accessed | tf_op | source)
XLA Modules:
  0.0 70.0 jit_solution(13165258502947736974)
XLA Ops:
  0.0 0.0 copy-start
  0.0 1.6 %copy-done = bf16[512,2048]{1,0:T(8,128)(2,1)S(1)} copy-done((bf16[512,2048]{1,0:T(8,128)(2,1)S(1)}, bf16[512,2048]{1,0:T(8,128)(2,1)}, u32[]{:S(2)}) %copy-start) | copy-done | bytes 2097176
  1.6 0.0 copy-start.1
  1.6 1.0 %copy-done.1 = f32[343,2,128]{2,1,0:T(2,128)S(1)} copy-done((f32[343,2,128]{2,1,0:T(2,128)S(1)}, f32[343,2,128]{2,1,0:T(2,128)}, u32[]{:S(2)}) %copy-start.1) | copy-done | bytes 351256
  2.6 0.0 copy-start.2
  2.6 0.9 %copy-done.2 = s32[1024,27]{0,1:T(8,128)S(1)} copy-done((s32[1024,27]{0,1:T(8,128)S(1)}, s32[1024,27]{0,1:T(8,128)}, u32[]{:S(2)}) %copy-start.2) | copy-done | bytes 110616
  3.5 0.0 copy-start.3
  3.5 0.9 %copy-done.3 = s32[1024,27]{0,1:T(8,128)S(1)} copy-done((s32[1024,27]{0,1:T(8,128)S(1)}, s32[1024,27]{0,1:T(8,128)}, u32[]{:S(2)}) %copy-start.3) | copy-done | bytes 110616
  4.4 0.0 copy-start.4
  4.4 0.8 %copy-done.4 = bf16[128,8,32]{0,2,1:T(8,128)(2,1)S(1)} copy-done((bf16[128,8,32]{0,2,1:T(8,128)(2,1)S(1)}, bf16[128,8,32]{0,2,1:T(8,128)(2,1)}, u32[]{:S(2)}) %copy-start.4) | copy-done | bytes 65560
  5.2 0.0 copy-start.5
  5.2 0.8 %copy-done.5 = f32[8,2048]{1,0:T(8,128)S(1)} copy-done((f32[8,2048]{1,0:T(8,128)S(1)}, f32[8,2048]{1,0:T(8,128)}, u32[]{:S(2)}) %copy-start.5) | copy-done | bytes 65560
  6.1 63.3 %shard_map.64 = bf16[256,128]{1,0:T(8,128)(2,1)S(1)} custom-call(bf16[256,128]{1,0:T(8,128)(2,1)S(1)} %bitcast.11, bf16[512,2048]{1,0:T(8,128)(2,1)S(1)} %copy-done, f32[8,2048]{1,0:T(8,128)S(1)} %copy-done.5, f32[343,2,128]{2,1,0:T(2,128)S(1)} %copy-done.1, s32[27,1024]{1,0:T(8,128)S(1)} %bitcast.9, s32[27,1024]{1,0:T(8,128)S(1)} %bitcast.10), custom_call_target="tpu_custom_call" | custom-call | tf_op jit(solution)/shard_map/pallas_call | solution.py:328
  69.4 0.6 copy.8
Async XLA Ops:
  0.0 1.6 %copy-start = (bf16[512,2048]{1,0:T(8,128)(2,1)S(1)}, bf16[512,2048]{1,0:T(8,128)(2,1)}, u32[]{:S(2)}) copy-start(bf16[512,2048]{1,0:T(8,128)(2,1)} %interp_hbm.1) | copy-start | bytes 6291460
  1.6 1.0 %copy-start.1 = (f32[343,2,128]{2,1,0:T(2,128)S(1)}, f32[343,2,128]{2,1,0:T(2,128)}, u32[]{:S(2)}) copy-start(f32[343,2,128]{2,1,0:T(2,128)} %trans_hbm.1) | copy-start | bytes 1053700
  2.6 0.9 %copy-start.2 = (s32[1024,27]{0,1:T(8,128)S(1)}, s32[1024,27]{0,1:T(8,128)}, u32[]{:S(2)}) copy-start(s32[1024,27]{0,1:T(8,128)} %param.10) | copy-start | bytes 331780
  3.5 0.9 %copy-start.3 = (s32[1024,27]{0,1:T(8,128)S(1)}, s32[1024,27]{0,1:T(8,128)}, u32[]{:S(2)}) copy-start(s32[1024,27]{0,1:T(8,128)} %param.11) | copy-start | bytes 331780
  4.4 0.8 %copy-start.4 = (bf16[128,8,32]{0,2,1:T(8,128)(2,1)S(1)}, bf16[128,8,32]{0,2,1:T(8,128)(2,1)}, u32[]{:S(2)}) copy-start(bf16[128,8,32]{0,2,1:T(8,128)(2,1)} %param.6) | copy-start | bytes 196612
  5.2 0.8 %copy-start.5 = (f32[8,2048]{1,0:T(8,128)S(1)}, f32[8,2048]{1,0:T(8,128)}, u32[]{:S(2)}) copy-start(f32[8,2048]{1,0:T(8,128)} %angle_hbm.1) | copy-start | bytes 196612

commit v2 on v1

v2 whole, which is shorter than its diff:
```python
import jax
import jax.numpy as jnp
from jax import lax
from jax.experimental import pallas as pl
from jax.experimental.pallas import tpu as pltpu
from jax.sharding import PartitionSpec as P

MESH = pl.DeviceIdType.MESH
F32 = jnp.float32
BF16 = jnp.bfloat16

NCD = 512
NPD = 2048
NBR = 27
NT = 343
NX = 8
NDIR = 16
RHS = 4
LAYERS = 4
BLK = 16
LANES = 128
PLANE = 64
GROUP = LAYERS * BLK
EDGE = 48
HALO = GROUP + 8 * EDGE
HALO_PAD = 512
NT_PAD = 384
STEP = 9
TURNS = [m for m in range(9) if m != 4]


def swap_lane_blocks(tiles):
    lane = lax.broadcasted_iota(jnp.int32, tiles[0].shape, 1)
    low = (lane // 32) % 2 == 0
    mid = (lane // 64) % 2 == 0
    v0, v1, v2, v3 = tiles

    def pair(a, b, keep, width):
        first = jnp.where(keep, a, pltpu.roll(b, width, 1))
        second = jnp.where(keep, pltpu.roll(a, LANES - width, 1), b)
        return first, second

    v0, v1 = pair(v0, v1, low, 32)
    v2, v3 = pair(v2, v3, low, 32)
    v0, v2 = pair(v0, v2, mid, 64)
    v1, v3 = pair(v1, v3, mid, 64)
    return [v0, v1, v2, v3]


def far_first(s):
    return 4 + (1 - 2 * (s % 2)) * ((s + 1) // 2)


def swap_parts(field, sign):
    part = (lax.broadcasted_iota(jnp.int32, field.shape, 0) // 2) % 2
    return jnp.where(part == 0, sign * pltpu.roll(field, 6, 0), -sign * pltpu.roll(field, 2, 0))


def kernel(
    child_hbm, interp_hbm, angle_hbm, trans_hbm, nidx_hbm, ntr_hbm, out_ref,
    child_v, interp_v, angle_v, trans_v, nidx_v, ntr_v,
    send_a, recv_a, lhs_v, cos_v, sin_v, send_p, recv_p, sum_v, field_v, turned_v, rows_v,
    pick_v, factor_v, table_hi, table_lo, send_q, recv_q, back_v, send_c, recv_c,
    load_sem, send_sem, recv_sem,
):
    box = lax.axis_index("box")
    me = lax.axis_index("dir")
    layer = box // 16
    zc = box % 16
    xb = zc % 2 + 2 * ((zc // 4) % 2)
    yb = (zc // 2) % 2 + 2 * (zc // 8)
    mx = me // 2
    half = me % 2
    my = half * 4 + layer

    def device(x, y):
        return ((y % 4) * 16 + zc, x * 2 + y // 4)

    def neighbour(m):
        dx, dy = m % 3 - 1, m // 3 - 1
        tx, ty = (xb - dx + 4) % 4, (yb - dy + 4) % 4
        return layer * 16 + tx % 2 + 2 * (ty % 2) + 4 * (tx // 2) + 8 * (ty // 2)

    def wait_for(ref, sem):
        pltpu.make_async_copy(ref, ref, sem).wait()

    barrier = pltpu.get_barrier_semaphore()

    def greet(t, carry):
        off = far_first(t)
        for to in (device((mx + off) % NX, my), device(mx, (my + off) % 8)):
            pl.semaphore_signal(barrier, inc=1, device_id=to, device_id_type=MESH)
        return carry

    lax.fori_loop(0, NX - 1, greet, 0)
    for m in TURNS:
        pl.semaphore_signal(barrier, inc=1, device_id=(neighbour(m), me), device_id_type=MESH)

    loads = [
        pltpu.make_async_copy(src, dst, load_sem.at[i])
        for i, (src, dst) in enumerate(
            [
                (child_hbm, child_v),
                (angle_hbm, angle_v),
                (nidx_hbm, nidx_v),
                (ntr_hbm, ntr_v),
                (interp_hbm.at[:, half], interp_v),
                (trans_hbm, trans_v),
            ]
        )
    ]
    for load in loads:
        load.start()

    loads[0].wait()
    for h in range(2):
        block = child_v[h * LANES : (h + 1) * LANES, :].astype(F32)
        send_a[:, h] = block.T.reshape(NX, 16, LANES).astype(BF16)

    pl.semaphore_wait(barrier, 2 * (NX - 1) + len(TURNS))

    def send_child(t, carry):
        to = (mx + far_first(t)) % NX
        pltpu.make_async_remote_copy(
            src_ref=send_a.at[to], dst_ref=recv_a.at[mx],
            send_sem=send_sem.at[0], recv_sem=recv_sem.at[0],
            device_id=device(to, my), device_id_type=MESH,
        ).start()
        return carry

    lax.fori_loop(0, NX - 1, send_child, 0)
    recv_a[mx] = send_a[mx]

    loads[1].wait()
    cos_v[...] = jnp.cos(angle_v[...])
    sin_v[...] = jnp.sin(angle_v[...])

    loads[2].wait()
    loads[3].wait()
    lane = lax.broadcasted_iota(jnp.int32, (32, LANES), 1)

    def mine(ref):
        parts = jnp.zeros((32, LANES), jnp.int32)
        for q in range(LAYERS):
            at = pl.multiple_of(q * 256 + (zc // 8) * LANES, LANES)
            cols = jnp.concatenate(
                [ref[:, pl.ds(at, LANES)], jnp.zeros((32 - NBR, LANES), jnp.int32)], axis=0
            )
            cols = pltpu.roll(cols, (q * BLK - (zc % 8) * BLK + LANES) % LANES, 1)
            parts = jnp.where(lane // BLK == q, cols, parts)
        return parts

    def to_rows(values, at):
        padded = jnp.concatenate([values.astype(F32), jnp.zeros((LANES - 32, LANES), F32)], axis=0)
        rows_v[at] = padded.T[0:GROUP, :]
        return jnp.concatenate([rows_v[at, pl.ds(i, GROUP // 2, stride=2), :] for i in range(2)], axis=0)

    source = mine(nidx_v)
    sx = source % 2 + 2 * ((source // 4) % 2) + 4 * ((source // 16) % 2) + 8 * ((source // 64) % 2)
    sy = (source // 2) % 2 + 2 * ((source // 8) % 2) + 4 * ((source // 32) % 2) + 8 * ((source // 128) % 2)
    sl = source // 256
    u = (sx - 4 * xb + 20) % 16
    v = (sy - 4 * yb + 20) % 16
    bx, x, by, y = u // 4, u % 4, v // 4, v % 4
    turn = by * 3 + bx
    base = GROUP + EDGE * (turn - (turn > 4).astype(jnp.int32))
    by_y = base + 16 * (y - (by == 0).astype(jnp.int32)) + 4 * x + sl
    by_x = base + 16 * (x - (bx == 0).astype(jnp.int32)) + 4 * y + sl
    row = jnp.where(by != 1, by_y, jnp.where(bx != 1, by_x, 16 * y + 4 * x + sl))
    source_rows = to_rows(row, 0)
    factor_rows = to_rows(mine(ntr_v), 1)

    slot_no = lax.broadcasted_iota(jnp.int32, (GROUP, HALO_PAD), 1).astype(F32)
    for n in range(NBR):
        pick_v[n * GROUP : (n + 1) * GROUP, :] = jnp.where(
            source_rows[:, n : n + 1] == slot_no, 1.0, 0.0
        ).astype(BF16)

    new = lax.broadcasted_iota(jnp.int32, (LANES, LANES), 0)
    old = lax.broadcasted_iota(jnp.int32, (LANES, LANES), 1)
    child_out_of = jnp.where((old % 8) * 16 + old // 8 == new, 1.0, 0.0).astype(BF16)
    child_into = jnp.where((new % 8) * 16 + new // 8 == old, 1.0, 0.0).astype(BF16)

    loads[4].wait()
    wait_for(recv_a.at[pl.ds(0, NX - 1)], recv_sem.at[0])
    columns = []
    for g in range(2):
        rows = [None] * 8
        for h in range(2):
            tiles = swap_lane_blocks([recv_a[4 * g + i, h].astype(F32) for i in range(4)])
            for c in range(RHS):
                rows[c * 2 + h] = tiles[c].astype(BF16)
        columns.append(jnp.concatenate(rows, axis=0))
    lhs_v[...] = jnp.dot(
        child_out_of, jnp.concatenate(columns, axis=1), preferred_element_type=F32
    ).astype(BF16)
    interp = interp_v[...].reshape(NCD // 2, NPD)
    for d2 in range(NDIR // 2):
        prod = jnp.dot(
            lhs_v[...], interp[:, d2 * 256 : (d2 + 1) * 256], preferred_element_type=F32
        )
        for i in range(2):
            d = d2 * 2 + i
            at = slice(d * LANES, (d + 1) * LANES)
            for w in range(2):
                by_cos = jnp.zeros((8, LANES), F32)
                by_sin = jnp.zeros((8, LANES), F32)
                for o in range(8):
                    part = prod[o * 16 + w * 8 : o * 16 + w * 8 + 8, i * LANES : (i + 1) * LANES]
                    by_cos = by_cos + part * cos_v[o : o + 1, at]
                    by_sin = by_sin + part * sin_v[o : o + 1, at]
                shifted = by_cos + swap_parts(by_sin, -1.0)
                for c in range(2):
                    send_p[d * RHS + w * 2 + c] = shifted[c * 4 : c * 4 + 4, :]

    my_slot = half * 32 + ((mx % 2 + 2 * (mx // 4)) * 2 + (mx // 2) % 2) * 4 + layer

    def target(t):
        return (mx + far_first(t // 8)) % NX, (my + far_first(t % 8)) % 8

    def send_parent(t, carry):
        tx, ty = target(t)
        pltpu.make_async_remote_copy(
            src_ref=send_p.at[(tx * 2 + ty // 4) * RHS + ty % 4], dst_ref=recv_p.at[my_slot],
            send_sem=send_sem.at[1], recv_sem=recv_sem.at[1],
            device_id=device(tx, ty), device_id_type=MESH,
        ).start()
        return carry

    lax.fori_loop(0, PLANE - 1, send_parent, 0)
    recv_p[my_slot] = send_p[me * RHS + layer]

    loads[5].wait()
    for h in range(2):
        values = trans_v[:, h, :]
        hi = values.astype(BF16)
        lo = (values - hi.astype(F32)).astype(BF16)
        pad = jnp.zeros((NT_PAD - NT, LANES), BF16)
        table_hi[:, h * LANES : (h + 1) * LANES] = jnp.concatenate([hi, pad], axis=0)
        table_lo[:, h * LANES : (h + 1) * LANES] = jnp.concatenate([lo, pad], axis=0)
    field_v[HALO:HALO_PAD, :] = jnp.zeros((HALO_PAD - HALO, 2 * LANES), BF16)

    wait_for(recv_p.at[pl.ds(0, PLANE - 1)], recv_sem.at[1])
    sum_v[...] = recv_p[0:32] + recv_p[32:64]
    for h in range(2):
        cols = slice(h * LANES, (h + 1) * LANES)

        def parents(gx, gy, h=h):
            first = (gy * 2 + gx // 2) * 4
            return sum_v[first : first + 4, h * 2 + gx % 2, :]

        field_v[0:GROUP, cols] = jnp.concatenate(
            [parents(gx, gy) for gy in range(4) for gx in range(4)], axis=0
        ).astype(BF16)
        turned_v[:, cols] = jnp.concatenate(
            [parents(gx, gy) for gx in range(4) for gy in range(4)], axis=0
        ).astype(BF16)

    for k, m in enumerate(TURNS):
        dx, dy = m % 3 - 1, m // 3 - 1
        first = 16 if (dy if dy else dx) < 0 else 0
        pltpu.make_async_remote_copy(
            src_ref=(field_v if dy else turned_v).at[pl.ds(first, EDGE)],
            dst_ref=field_v.at[pl.ds(GROUP + EDGE * k, EDGE)],
            send_sem=send_sem.at[2], recv_sem=recv_sem.at[2],
            device_id=(neighbour(m), me), device_id_type=MESH,
        ).start()

    factor_no = lax.broadcasted_iota(jnp.int32, (GROUP, NT_PAD), 1).astype(F32)
    for s in range(0, NBR, STEP):
        chosen = jnp.concatenate(
            [
                jnp.where(factor_rows[:, n : n + 1] == factor_no, 1.0, 0.0).astype(BF16)
                for n in range(s, s + STEP)
            ],
            axis=0,
        )
        factor_v[s * GROUP : (s + STEP) * GROUP, :] = jnp.dot(
            chosen, table_hi[...], preferred_element_type=F32
        ) + jnp.dot(chosen, table_lo[...], preferred_element_type=F32)

    wait_for(field_v.at[pl.ds(GROUP, 8 * EDGE)], recv_sem.at[2])
    sum_re = jnp.zeros((GROUP, LANES), F32)
    sum_im = jnp.zeros((GROUP, LANES), F32)
    for s in range(0, NBR, STEP):
        picked = jnp.dot(
            pick_v[s * GROUP : (s + STEP) * GROUP, :], field_v[...], preferred_element_type=F32
        )
        for n in range(STEP):
            re = picked[n * GROUP : (n + 1) * GROUP, 0:LANES]
            im = picked[n * GROUP : (n + 1) * GROUP, LANES : 2 * LANES]
            at = (s + n) * GROUP
            t_re = factor_v[at : at + GROUP, 0:LANES]
            t_im = factor_v[at : at + GROUP, LANES : 2 * LANES]
            sum_re = sum_re + (re * t_re - im * t_im)
            sum_im = sum_im + (re * t_im + im * t_re)
    for h, total in enumerate((sum_re, sum_im)):
        total = total.astype(BF16).astype(F32)
        for i in range(2):
            send_q[:, h * 2 + i, :] = total[i * 32 : (i + 1) * 32, :]

    my_piece = me * RHS + layer

    def send_sum(t, carry):
        tx, ty = target(t)
        pltpu.make_async_remote_copy(
            src_ref=send_q.at[(ty % 4) * NX + tx], dst_ref=recv_q.at[my_piece],
            send_sem=send_sem.at[3], recv_sem=recv_sem.at[3],
            device_id=device(tx, ty), device_id_type=MESH,
        ).start()
        return carry

    lax.fori_loop(0, PLANE - 1, send_sum, 0)
    recv_q[my_piece] = send_q[layer * NX + mx]

    wait_for(recv_q.at[pl.ds(0, PLANE - 1)], recv_sem.at[3])
    for d in range(NDIR):
        at = slice(d * LANES, (d + 1) * LANES)
        fields = []
        for w in range(2):
            first = d * RHS + 2 * w
            field = jnp.concatenate([recv_q[first], recv_q[first + 1]], axis=0)
            fields.append((field, swap_parts(field, 1.0)))
        for o in range(8):
            cosine = cos_v[o : o + 1, at]
            sine = sin_v[o : o + 1, at]
            back_v[o * 16 : (o + 1) * 16, at] = jnp.concatenate(
                [field * cosine + turned * sine for field, turned in fields], axis=0
            ).astype(BF16)
    prod = 0.125 * lax.dot_general(
        back_v[...], interp, (((1,), (1,)), ((), ())), preferred_element_type=F32
    )
    prod = jnp.dot(child_into, prod.astype(BF16), preferred_element_type=F32)
    for g in range(2):
        for h in range(2):
            tiles = swap_lane_blocks(
                [
                    prod[c * 32 + h * 16 : c * 32 + h * 16 + 16, g * LANES : (g + 1) * LANES]
                    for c in range(RHS)
                ]
            )
            for i in range(4):
                send_c[4 * g + i, h] = tiles[i].astype(BF16)

    def send_result(t, carry):
        to = (mx + far_first(t)) % NX
        pltpu.make_async_remote_copy(
            src_ref=send_c.at[to], dst_ref=recv_c.at[mx],
            send_sem=send_sem.at[4], recv_sem=recv_sem.at[4],
            device_id=device(to, my), device_id_type=MESH,
        ).start()
        return carry

    lax.fori_loop(0, NX - 1, send_result, 0)
    recv_c[mx] = send_c[mx]
    wait_for(recv_c.at[pl.ds(0, NX - 1)], recv_sem.at[4])
    for h in range(2):
        block = recv_c[:, h].astype(F32).reshape(LANES, LANES)
        out_ref[h * LANES : (h + 1) * LANES, :] = block.T.astype(BF16)

    wait_for(send_a.at[pl.ds(0, NX - 1)], send_sem.at[0])
    wait_for(send_p.at[pl.ds(0, PLANE - 1)], send_sem.at[1])
    wait_for(field_v.at[pl.ds(0, 8 * EDGE)], send_sem.at[2])
    wait_for(recv_q.at[pl.ds(0, PLANE - 1)], send_sem.at[3])
    wait_for(send_c.at[pl.ds(0, NX - 1)], send_sem.at[4])


def per_device(child_out, interp, shift_angle, translators, nbr_index, nbr_trans):
    count, cols, width = child_out.shape
    children = child_out.transpose(1, 2, 0).reshape(cols * width, count)
    out = pl.pallas_call(
        kernel,
        out_shape=jax.ShapeDtypeStruct((cols * width, count), BF16),
        in_specs=[pl.BlockSpec(memory_space=pl.ANY)] * 6,
        out_specs=pl.BlockSpec(memory_space=pltpu.VMEM),
        scratch_shapes=[
            pltpu.VMEM((cols * width, count), BF16),
            pltpu.VMEM((NX, 32, NPD), BF16),
            pltpu.VMEM((8, NPD), F32),
            pltpu.VMEM((NT, 2, LANES), F32),
            pltpu.VMEM((NBR, 1024), jnp.int32),
            pltpu.VMEM((NBR, 1024), jnp.int32),
            pltpu.VMEM((NX, 2, 16, LANES), BF16),
            pltpu.VMEM((NX, 2, 16, LANES), BF16),
            pltpu.VMEM((LANES, NCD // 2), BF16),
            pltpu.VMEM((8, NPD), F32),
            pltpu.VMEM((8, NPD), F32),
            pltpu.VMEM((PLANE, 4, LANES), F32),
            pltpu.VMEM((PLANE, 4, LANES), F32),
            pltpu.VMEM((PLANE // 2, 4, LANES), F32),
            pltpu.VMEM((HALO_PAD, 2 * LANES), BF16),
            pltpu.VMEM((GROUP, 2 * LANES), BF16),
            pltpu.VMEM((2, GROUP, LANES), F32),
            pltpu.VMEM((NBR * GROUP, HALO_PAD), BF16),
            pltpu.VMEM((NBR * GROUP, 2 * LANES), F32),
            pltpu.VMEM((NT_PAD, 2 * LANES), BF16),
            pltpu.VMEM((NT_PAD, 2 * LANES), BF16),
            pltpu.VMEM((PLANE // 2, 4, LANES), F32),
            pltpu.VMEM((PLANE, 4, LANES), F32),
            pltpu.VMEM((LANES, NPD), BF16),
            pltpu.VMEM((NX, 2, 16, LANES), BF16),
            pltpu.VMEM((NX, 2, 16, LANES), BF16),
            pltpu.SemaphoreType.DMA((6,)),
            pltpu.SemaphoreType.DMA((5,)),
            pltpu.SemaphoreType.DMA((5,)),
        ],
        compiler_params=pltpu.CompilerParams(
            collective_id=0, has_side_effects=True, vmem_limit_bytes=60 * 1024 * 1024
        ),
    )(
        children,
        interp.reshape(NX, 2, 32, NPD),
        shift_angle,
        translators,
        nbr_index.T,
        nbr_trans.T,
    )
    return out.reshape(cols, width, count).transpose(2, 0, 1)


def solution(mesh):
    return jax.shard_map(
        per_device,
        mesh=mesh,
        in_specs=(P("box", None, "dir"), P(), P(), P(None, None, "dir"), P(), P()),
        out_specs=P("box", None, "dir"),
        check_vma=False,
    )
```

time: 70.4 us -> 57 us (0.81)
  Pallas kernels: 63.3 us -> 55.1 us
  local copies, waits for them, and re-layouts: 6.69 us -> 1.47 us
    pallas_call x1, Pallas kernels: 63.3 us -> 55.1 us  [per_device(): pl.pallas_call(kernel, out_shape=jax.ShapeDtypeStruct((cols * width, coun...]
    unnamed x13 -> x1, local copies, waits for them, and re-layouts: 6.69 us -> 1.47 us
where the time goes in v2:
time: 57 us; the launch traced here: 56.6 us
  Pallas kernels  55.1 us (97%)
  local copies, waits for them, and re-layouts  1.47 us (3%)
    pallas_call x1, Pallas kernels, per_device(): pl.pallas_call(kernel, out_shape=jax.ShapeDtypeStruct((cols * width, coun...  55.1 us
    unnamed x1, local copies, waits for them, and re-layouts  1.47 us

profile of v2, /device:TPU:1, one launch (start us, length us, event | category | flops | bytes accessed | tf_op | source)
XLA Modules:
  0.0 56.6 jit_solution(1012586730475016944)
XLA Ops:
  0.0 55.1 %shard_map.64 = bf16[256,128]{1,0:T(8,128)(2,1)} custom-call(bf16[256,128]{1,0:T(8,128)(2,1)} %bitcast.13, bf16[8,2,32,2048]{3,2,1,0:T(8,128)(2,1)} %bitcast.9, f32[8,2048]{1,0:T(8,128)} %angle_hbm.1, f32[343,2,128]{2,1,0:T(2,128)} %trans_hbm.1, s32[27,1024]{1,0:T(8,128)} %bitcast.11, s32[27,1024]{1,0:T(8,128)} %bitcast.12), custom_call_target="tpu_custom_call" | custom-call | tf_op jit(solution)/shard_map/pallas_call | solution.py:371
  55.1 1.5 %copy.8 = bf16[128,8,32]{0,2,1:T(8,128)(2,1)} copy(bf16[128,8,32]{0,2,1:T(8,128)(2,1)} %bitcast.10) | data formatting | bytes 131072

commit v3 on v2

v3 whole, which is shorter than its diff:
```python
import jax
import jax.numpy as jnp
from jax import lax
from jax.experimental import pallas as pl
from jax.experimental.pallas import tpu as pltpu
from jax.sharding import PartitionSpec as P

MESH = pl.DeviceIdType.MESH
F32 = jnp.float32
BF16 = jnp.bfloat16

NCD = 512
NPD = 2048
NBR = 27
NT = 343
NX = 8
NY = 8
WIDE = NPD // 2
RHS = 4
LAYERS = 4
BLK = 16
LANES = 128
GROUP = LAYERS * BLK
EDGE = 48
HALO = GROUP + 8 * EDGE
HALO_PAD = 512
NT_SENT = 352
NT_PAD = 384
STEP = 9
TURNS = [m for m in range(9) if m != 4]


def far_first(s):
    return 4 + (1 - 2 * (s % 2)) * ((s + 1) // 2)


def kernel(
    child_hbm, interp_hbm, angle_hbm, trans_hbm, nidx_hbm, ntr_hbm, out_ref,
    interp_v, angle_v, trans_v, nidx_v, ntr_v,
    recv_a, cos_v, sin_v, table_out, table_v, send_b, recv_b, field_v, turned_v,
    pick_v, factor_v, send_d, recv_d, parent_v, back_v, send_e, recv_e,
    load_sem, send_sem, recv_sem,
):
    box = lax.axis_index("box")
    me = lax.axis_index("dir")
    layer = box // 16
    zc = box % 16
    xb = zc % 2 + 2 * ((zc // 4) % 2)
    yb = (zc // 2) % 2 + 2 * (zc // 8)
    mx = me // 2
    half = me % 2
    my = half * 4 + layer

    def device(x, y):
        return ((y % 4) * 16 + zc, x * 2 + y // 4)

    def neighbour(m):
        dx, dy = m % 3 - 1, m // 3 - 1
        tx, ty = (xb - dx + 4) % 4, (yb - dy + 4) % 4
        return layer * 16 + tx % 2 + 2 * (ty % 2) + 4 * (tx // 2) + 8 * (ty // 2)

    def wait_for(ref, sem):
        pltpu.make_async_copy(ref, ref, sem).wait()

    def send(src, dst, phase, to):
        return pltpu.make_async_remote_copy(
            src_ref=src, dst_ref=dst, send_sem=send_sem.at[phase], recv_sem=recv_sem.at[phase],
            device_id=to, device_id_type=MESH,
        )

    barrier = pltpu.get_barrier_semaphore()

    def greet(t, carry):
        off = far_first(t)
        for to in (device((mx + off) % NX, my), device(mx, (my + off) % NY)):
            pl.semaphore_signal(barrier, inc=1, device_id=to, device_id_type=MESH)
        return carry

    lax.fori_loop(0, NX - 1, greet, 0)
    for m in TURNS:
        pl.semaphore_signal(barrier, inc=1, device_id=(neighbour(m), me), device_id_type=MESH)

    copies = [
        (child_hbm.at[:, mx % 4], recv_a.at[mx]),
        (trans_hbm, trans_v),
        (nidx_hbm, nidx_v),
        (ntr_hbm, ntr_v),
    ]
    for q in range(LAYERS):
        at = pl.ds(pl.multiple_of((mx + 7 + q) % NX * 256, 256), 256)
        to = pl.ds(q * 256, 256)
        copies.append((angle_hbm.at[:, at], angle_v.at[:, to]))
        copies.append((interp_hbm.at[:, half, :, at], interp_v.at[:, :, to]))
    loads = [pltpu.make_async_copy(src, dst, load_sem.at[i]) for i, (src, dst) in enumerate(copies)]
    for load in loads:
        load.start()

    pl.semaphore_wait(barrier, (NX - 1) + (NY - 1) + len(TURNS))

    def send_child(t, carry):
        to = (mx + far_first(t)) % NX
        send(child_hbm.at[:, to % 4], recv_a.at[mx], 0, device(to, my)).start()
        return carry

    lax.fori_loop(0, NX - 1, send_child, 0)

    loads[1].wait()
    for h in range(2):
        table_out[:, h * LANES : (h + 1) * LANES] = jnp.concatenate(
            [trans_v[:, h, :], jnp.zeros((NT_SENT - NT, LANES), F32)], axis=0
        ).astype(BF16)
    table_v[NT_SENT:NT_PAD, :] = jnp.zeros((NT_PAD - NT_SENT, 2 * LANES), BF16)
    table_in = table_v.at[pl.ds(0, NT_SENT)]
    send_table = send(table_out, table_in, 5, device((mx + 9 - layer) % NX, my))

    @pl.when(layer != 1)
    def _():
        send_table.start()

    @pl.when(layer == 1)
    def _():
        pltpu.make_async_copy(table_out, table_in, recv_sem.at[5]).start()

    for q in range(LAYERS):
        loads[4 + 2 * q].wait()
    cos_v[...] = jnp.cos(angle_v[...])
    sin_v[...] = jnp.sin(angle_v[...])

    loads[2].wait()
    loads[3].wait()
    lane = lax.broadcasted_iota(jnp.int32, (32, LANES), 1)

    def mine(ref):
        parts = jnp.zeros((32, LANES), jnp.int32)
        for q in range(LAYERS):
            at = pl.multiple_of(q * 256 + (zc // 8) * LANES, LANES)
            cols = jnp.concatenate(
                [ref[:, pl.ds(at, LANES)], jnp.zeros((32 - NBR, LANES), jnp.int32)], axis=0
            )
            cols = pltpu.roll(cols, (q * BLK - (zc % 8) * BLK + LANES) % LANES, 1)
            parts = jnp.where(lane // BLK == q, cols, parts)
        return parts

    source = mine(nidx_v)
    sx = source % 2 + 2 * ((source // 4) % 2) + 4 * ((source // 16) % 2) + 8 * ((source // 64) % 2)
    sy = (source // 2) % 2 + 2 * ((source // 8) % 2) + 4 * ((source // 32) % 2) + 8 * ((source // 128) % 2)
    sl = source // 256
    u = (sx - 4 * xb + 20) % 16
    v = (sy - 4 * yb + 20) % 16
    bx, x, by, y = u // 4, u % 4, v // 4, v % 4
    turn = by * 3 + bx
    base = GROUP + EDGE * (turn - (turn > 4).astype(jnp.int32))
    by_y = base + 16 * (y - (by == 0).astype(jnp.int32)) + 4 * x + sl
    by_x = base + 16 * (x - (bx == 0).astype(jnp.int32)) + 4 * y + sl
    row = jnp.where(by != 1, by_y, jnp.where(bx != 1, by_x, 16 * y + 4 * x + sl))
    source_rows = row.astype(F32).T[0:GROUP, :]
    factor_rows = mine(ntr_v).astype(F32).T[0:GROUP, :]

    slot_no = lax.broadcasted_iota(jnp.int32, (GROUP, HALO_PAD), 1).astype(F32)
    for n in range(NBR):
        pick_v[n * GROUP : (n + 1) * GROUP, :] = jnp.where(
            source_rows[:, n : n + 1] == slot_no, 1.0, 0.0
        ).astype(BF16)
    field_v[HALO:HALO_PAD, :] = jnp.zeros((HALO_PAD - HALO, 2 * LANES), BF16)

    new = lax.broadcasted_iota(jnp.int32, (LANES, LANES), 0)
    old = lax.broadcasted_iota(jnp.int32, (LANES, LANES), 1)
    by_child = jnp.where((old % 8) * 16 + old // 8 == new, 1.0, 0.0).astype(BF16)
    new = lax.broadcasted_iota(jnp.int32, (2 * GROUP, GROUP), 0)
    old = lax.broadcasted_iota(jnp.int32, (2 * GROUP, GROUP), 1)
    px = old % 2 + 2 * ((old // 4) % 2)
    py = (old // 2) % 2 + 2 * ((old // 8) % 2)
    straight = 16 * py + 4 * px + old // 16
    turned = GROUP + 16 * px + 4 * py + old // 16
    in_order = jnp.where((straight == new) | (turned == new), 1.0, 0.0).astype(BF16)

    for q in range(LAYERS):
        loads[5 + 2 * q].wait()
    loads[0].wait()
    wait_for(recv_a.at[pl.ds(0, NX - 1)], recv_sem.at[0])
    children = jnp.concatenate(
        [
            lax.dot_general(
                by_child, recv_a[:, h].reshape(NCD // 2, LANES), (((1,), (1,)), ((), ())),
                preferred_element_type=F32,
            ).astype(BF16)
            for h in range(2)
        ],
        axis=0,
    )
    interp = interp_v[...].reshape(NCD // 2, WIDE)
    for q in range(LAYERS):
        prod = jnp.dot(
            children, interp[:, q * 256 : (q + 1) * 256], preferred_element_type=F32
        )
        for i in range(2):
            at = slice(q * 256 + i * LANES, q * 256 + (i + 1) * LANES)
            total_re = jnp.zeros((BLK, LANES), F32)
            total_im = jnp.zeros((BLK, LANES), F32)
            for o in range(8):
                re = prod[o * BLK : (o + 1) * BLK, i * LANES : (i + 1) * LANES]
                im = prod[LANES + o * BLK : LANES + (o + 1) * BLK, i * LANES : (i + 1) * LANES]
                cosine = cos_v[o : o + 1, at]
                sine = sin_v[o : o + 1, at]
                total_re = total_re + (re * cosine - im * sine)
                total_im = total_im + (re * sine + im * cosine)
            send_b[i * 4 + q, 0] = total_re.astype(BF16)
            send_b[i * 4 + q, 1] = total_im.astype(BF16)

            @pl.when(i * 4 + q != my)
            def _(to=i * 4 + q):
                send(send_b.at[to], recv_b.at[my], 1, device(mx, to)).start()

    recv_b[my] = send_b[my]

    wait_for(recv_b.at[pl.ds(0, NY - 1)], recv_sem.at[1])
    whole = (recv_b[0:4].astype(F32) + recv_b[4:8].astype(F32)).astype(BF16)
    whole = jnp.concatenate([whole[:, h].reshape(GROUP, LANES) for h in range(2)], axis=1)
    ordered = jnp.dot(in_order, whole, preferred_element_type=F32).astype(BF16)
    field_v[0:GROUP, :] = ordered[0:GROUP]
    turned_v[...] = ordered[GROUP : 2 * GROUP]

    for k, m in enumerate(TURNS):
        dx, dy = m % 3 - 1, m // 3 - 1
        first = 16 if (dy if dy else dx) < 0 else 0
        send(
            (field_v if dy else turned_v).at[pl.ds(first, EDGE)],
            field_v.at[pl.ds(GROUP + EDGE * k, EDGE)],
            2,
            (neighbour(m), me),
        ).start()

    wait_for(table_in, recv_sem.at[5])
    factor_no = lax.broadcasted_iota(jnp.int32, (GROUP, NT_PAD), 1).astype(F32)
    for s in range(0, NBR, STEP):
        chosen = jnp.concatenate(
            [
                jnp.where(factor_rows[:, n : n + 1] == factor_no, 1.0, 0.0).astype(BF16)
                for n in range(s, s + STEP)
            ],
            axis=0,
        )
        factor_v[s * GROUP : (s + STEP) * GROUP, :] = jnp.dot(
            chosen, table_v[...], preferred_element_type=F32
        )

    wait_for(field_v.at[pl.ds(GROUP, 8 * EDGE)], recv_sem.at[2])
    sum_re = jnp.zeros((GROUP, LANES), F32)
    sum_im = jnp.zeros((GROUP, LANES), F32)
    for s in range(0, NBR, STEP):
        picked = jnp.dot(
            pick_v[s * GROUP : (s + STEP) * GROUP, :], field_v[...], preferred_element_type=F32
        )
        for n in range(STEP):
            re = picked[n * GROUP : (n + 1) * GROUP, 0:LANES]
            im = picked[n * GROUP : (n + 1) * GROUP, LANES : 2 * LANES]
            at = (s + n) * GROUP
            t_re = factor_v[at : at + GROUP, 0:LANES]
            t_im = factor_v[at : at + GROUP, LANES : 2 * LANES]
            sum_re = sum_re + (re * t_re - im * t_im)
            sum_im = sum_im + (re * t_im + im * t_re)
    for h, total in enumerate((sum_re, sum_im)):
        send_d[:, h] = total.astype(BF16).reshape(LAYERS, BLK, LANES)

    def send_sum(t, carry):
        to = (my + far_first(t)) % NY
        send(send_d.at[to % 4], recv_d.at[my], 3, device(mx, to)).start()
        return carry

    lax.fori_loop(0, NY - 1, send_sum, 0)
    recv_d[my] = send_d[layer]

    wait_for(recv_d.at[pl.ds(0, NY - 1)], recv_sem.at[3])
    parent_v[...] = recv_d[...].astype(F32)
    for i in range(2):
        for q in range(LAYERS):
            at = slice(q * 256 + i * LANES, q * 256 + (i + 1) * LANES)
            cosine = cos_v[:, at]
            sine = sin_v[:, at]
            for p in range(0, BLK, 2):
                backs = [[], []]
                for r in range(p, p + 2):
                    re = parent_v[i * 4 + q, 0, r : r + 1, :]
                    im = parent_v[i * 4 + q, 1, r : r + 1, :]
                    backs[0].append(re * cosine + im * sine)
                    backs[1].append(im * cosine - re * sine)
                for h in range(2):
                    first = h * LANES + p * 8
                    back_v[first : first + 16, at] = jnp.concatenate(backs[h], axis=0).astype(BF16)
    prod = 0.125 * lax.dot_general(
        interp, back_v[...], (((1,), (1,)), ((), ())), preferred_element_type=F32
    )
    for h in range(2):
        send_e[:, h] = prod[:, h * LANES : (h + 1) * LANES].astype(BF16).reshape(NX, 32, LANES)

    def send_result(t, carry):
        to = (mx + far_first(t)) % NX
        send(send_e.at[to], recv_e.at[mx], 4, device(to, my)).start()
        return carry

    lax.fori_loop(0, NX - 1, send_result, 0)
    recv_e[mx] = send_e[mx]
    wait_for(recv_e.at[pl.ds(0, NX - 1)], recv_sem.at[4])
    for h in range(2):
        for c in range(RHS):
            first = h * LANES + c * 32
            out_ref[first : first + 32, :] = (
                recv_e[c, h].astype(F32) + recv_e[c + 4, h].astype(F32)
            ).astype(BF16)

    wait_for(recv_a.at[pl.ds(0, NX - 1)], send_sem.at[0])
    wait_for(send_b.at[pl.ds(0, NY - 1)], send_sem.at[1])
    wait_for(field_v.at[pl.ds(0, 8 * EDGE)], send_sem.at[2])
    wait_for(recv_d.at[pl.ds(0, NY - 1)], send_sem.at[3])
    wait_for(send_e.at[pl.ds(0, NX - 1)], send_sem.at[4])

    @pl.when(layer != 1)
    def _():
        wait_for(table_out, send_sem.at[5])


def per_device(child_out, interp, shift_angle, translators, nbr_index, nbr_trans):
    count, cols, width = child_out.shape
    children = child_out.transpose(1, 2, 0).reshape(2, RHS, width, count)
    out = pl.pallas_call(
        kernel,
        out_shape=jax.ShapeDtypeStruct((cols * width, count), BF16),
        in_specs=[pl.BlockSpec(memory_space=pl.ANY)] * 6,
        out_specs=pl.BlockSpec(memory_space=pltpu.VMEM),
        scratch_shapes=[
            pltpu.VMEM((NX, 32, WIDE), BF16),
            pltpu.VMEM((8, WIDE), F32),
            pltpu.VMEM((NT, 2, LANES), F32),
            pltpu.VMEM((NBR, 1024), jnp.int32),
            pltpu.VMEM((NBR, 1024), jnp.int32),
            pltpu.VMEM((NX, 2, 32, LANES), BF16),
            pltpu.VMEM((8, WIDE), F32),
            pltpu.VMEM((8, WIDE), F32),
            pltpu.VMEM((NT_SENT, 2 * LANES), BF16),
            pltpu.VMEM((NT_PAD, 2 * LANES), BF16),
            pltpu.VMEM((NY, 2, BLK, LANES), BF16),
            pltpu.VMEM((NY, 2, BLK, LANES), BF16),
            pltpu.VMEM((HALO_PAD, 2 * LANES), BF16),
            pltpu.VMEM((GROUP, 2 * LANES), BF16),
            pltpu.VMEM((NBR * GROUP, HALO_PAD), BF16),
            pltpu.VMEM((NBR * GROUP, 2 * LANES), F32),
            pltpu.VMEM((LAYERS, 2, BLK, LANES), BF16),
            pltpu.VMEM((NY, 2, BLK, LANES), BF16),
            pltpu.VMEM((NY, 2, BLK, LANES), F32),
            pltpu.VMEM((2 * LANES, WIDE), BF16),
            pltpu.VMEM((NX, 2, 32, LANES), BF16),
            pltpu.VMEM((NX, 2, 32, LANES), BF16),
            pltpu.SemaphoreType.DMA((12,)),
            pltpu.SemaphoreType.DMA((6,)),
            pltpu.SemaphoreType.DMA((6,)),
        ],
        compiler_params=pltpu.CompilerParams(
            collective_id=0, has_side_effects=True, vmem_limit_bytes=60 * 1024 * 1024
        ),
    )(
        children,
        interp.reshape(NX, 2, 32, NPD),
        shift_angle,
        translators,
        nbr_index.T,
        nbr_trans.T,
    )
    return out.reshape(cols, width, count).transpose(2, 0, 1)


def solution(mesh):
    return jax.shard_map(
        per_device,
        mesh=mesh,
        in_specs=(P("box", None, "dir"), P(), P(), P(None, None, "dir"), P(), P()),
        out_specs=P("box", None, "dir"),
        check_vma=False,
    )
```

time: 57 us -> 52 us (0.912)
  Pallas kernels: 55.1 us -> 50.4 us
    pallas_call x1, Pallas kernels: 55.1 us -> 50.4 us  [per_device(): pl.pallas_call(kernel, out_shape=jax.ShapeDtypeStruct((cols * width, coun...]
where the time goes in v3:
time: 52 us; the launch traced here: 51.9 us
  Pallas kernels  50.4 us (97%)
  local copies, waits for them, and re-layouts  1.47 us (3%)
    pallas_call x1, Pallas kernels, per_device(): pl.pallas_call(kernel, out_shape=jax.ShapeDtypeStruct((cols * width, coun...  50.4 us
    unnamed x1, local copies, waits for them, and re-layouts  1.47 us

profile of v3, /device:TPU:1, one launch (start us, length us, event | category | flops | bytes accessed | tf_op | source)
XLA Modules:
  0.0 51.9 jit_solution(14820833710656856018)
XLA Ops:
  0.0 50.4 %shard_map.64 = bf16[256,128]{1,0:T(8,128)(2,1)} custom-call(bf16[2,4,32,128]{3,2,1,0:T(8,128)(2,1)} %bitcast.13, bf16[8,2,32,2048]{3,2,1,0:T(8,128)(2,1)} %bitcast.9, f32[8,2048]{1,0:T(8,128)} %angle_hbm.1, f32[343,2,128]{2,1,0:T(2,128)} %trans_hbm.1, s32[27,1024]{1,0:T(8,128)} %bitcast.11, s32[27,1024]{1,0:T(8,128)} %bitcast.12), custom_call_target="tpu_custom_call" | custom-call | tf_op jit(solution)/shard_map/pallas_call | solution.py:325
  50.4 1.5 %copy.8 = bf16[128,8,32]{0,2,1:T(8,128)(2,1)} copy(bf16[128,8,32]{0,2,1:T(8,128)(2,1)} %bitcast.10) | data formatting | bytes 131072

commit v4 on v3

--- a/solution.py
+++ b/solution.py
@@ -36,7 +36,7 @@
 
 def kernel(
     child_hbm, interp_hbm, angle_hbm, trans_hbm, nidx_hbm, ntr_hbm, out_ref,
-    interp_v, angle_v, trans_v, nidx_v, ntr_v,
+    child_v, interp_v, angle_v, trans_v, nidx_v, ntr_v,
     recv_a, cos_v, sin_v, table_out, table_v, send_b, recv_b, field_v, turned_v,
     pick_v, factor_v, send_d, recv_d, parent_v, back_v, send_e, recv_e,
     load_sem, send_sem, recv_sem,
@@ -81,7 +81,7 @@
         pl.semaphore_signal(barrier, inc=1, device_id=(neighbour(m), me), device_id_type=MESH)
 
     copies = [
-        (child_hbm.at[:, mx % 4], recv_a.at[mx]),
+        (child_hbm, child_v),
         (trans_hbm, trans_v),
         (nidx_hbm, nidx_v),
         (ntr_hbm, ntr_v),
@@ -95,11 +95,13 @@
     for load in loads:
         load.start()
 
+    loads[0].wait()
+    recv_a[mx] = child_v[:, mx % 4]
     pl.semaphore_wait(barrier, (NX - 1) + (NY - 1) + len(TURNS))
 
     def send_child(t, carry):
         to = (mx + far_first(t)) % NX
-        send(child_hbm.at[:, to % 4], recv_a.at[mx], 0, device(to, my)).start()
+        send(child_v.at[:, to % 4], recv_a.at[mx], 0, device(to, my)).start()
         return carry
 
     lax.fori_loop(0, NX - 1, send_child, 0)
@@ -111,16 +113,6 @@
         ).astype(BF16)
     table_v[NT_SENT:NT_PAD, :] = jnp.zeros((NT_PAD - NT_SENT, 2 * LANES), BF16)
     table_in = table_v.at[pl.ds(0, NT_SENT)]
-    send_table = send(table_out, table_in, 5, device((mx + 9 - layer) % NX, my))
-
-    @pl.when(layer != 1)
-    def _():
-        send_table.start()
-
-    @pl.when(layer == 1)
-    def _():
-        pltpu.make_async_copy(table_out, table_in, recv_sem.at[5]).start()
-
     for q in range(LAYERS):
         loads[4 + 2 * q].wait()
     cos_v[...] = jnp.cos(angle_v[...])
@@ -176,8 +168,17 @@
 
     for q in range(LAYERS):
         loads[5 + 2 * q].wait()
-    loads[0].wait()
     wait_for(recv_a.at[pl.ds(0, NX - 1)], recv_sem.at[0])
+    send_table = send(table_out, table_in, 5, device((mx + 9 - layer) % NX, my))
+
+    @pl.when(layer != 1)
+    def _():
+        send_table.start()
+
+    @pl.when(layer == 1)
+    def _():
+        pltpu.make_async_copy(table_out, table_in, recv_sem.at[5]).start()
+
     children = jnp.concatenate(
         [
             lax.dot_general(
@@ -188,20 +189,19 @@
         ],
         axis=0,
     )
-    interp = interp_v[...].reshape(NCD // 2, WIDE)
-    for q in range(LAYERS):
-        prod = jnp.dot(
-            children, interp[:, q * 256 : (q + 1) * 256], preferred_element_type=F32
-        )
+    for turn in (0, 3, 1, 2):
+        q = (layer + turn) % LAYERS
+        some = interp_v[:, :, pl.ds(pl.multiple_of(q * 256, 256), 256)]
+        prod = jnp.dot(children, some.reshape(NCD // 2, 256), preferred_element_type=F32)
         for i in range(2):
-            at = slice(q * 256 + i * LANES, q * 256 + (i + 1) * LANES)
+            at = pl.ds(pl.multiple_of(q * 256 + i * LANES, LANES), LANES)
             total_re = jnp.zeros((BLK, LANES), F32)
             total_im = jnp.zeros((BLK, LANES), F32)
             for o in range(8):
                 re = prod[o * BLK : (o + 1) * BLK, i * LANES : (i + 1) * LANES]
                 im = prod[LANES + o * BLK : LANES + (o + 1) * BLK, i * LANES : (i + 1) * LANES]
-                cosine = cos_v[o : o + 1, at]
-                sine = sin_v[o : o + 1, at]
+                cosine = cos_v[pl.ds(o, 1), at]
+                sine = sin_v[pl.ds(o, 1), at]
                 total_re = total_re + (re * cosine - im * sine)
                 total_im = total_im + (re * sine + im * cosine)
             send_b[i * 4 + q, 0] = total_re.astype(BF16)
@@ -220,12 +220,16 @@
     field_v[0:GROUP, :] = ordered[0:GROUP]
     turned_v[...] = ordered[GROUP : 2 * GROUP]
 
-    for k, m in enumerate(TURNS):
-        dx, dy = m % 3 - 1, m // 3 - 1
-        first = 16 if (dy if dy else dx) < 0 else 0
+    for fx, fy in ((3, 3), (0, 3), (1, 3), (3, 1), (3, 0), (0, 1), (1, 1), (1, 0)):
+        dx = (1 if fx == 3 else -1) * (1 - 2 * (xb % 2)) if fx else 0
+        dy = (1 if fy == 3 else -1) * (1 - 2 * (yb % 2)) if fy else 0
+        m = (dy + 1) * 3 + dx + 1
+        slot = m - (m + 4) // 9
+        first = pl.multiple_of(8 - 8 * (dy if fy else dx), 16)
+        at = pl.multiple_of(GROUP + EDGE * slot, 16)
         send(
-            (field_v if dy else turned_v).at[pl.ds(first, EDGE)],
-            field_v.at[pl.ds(GROUP + EDGE * k, EDGE)],
+            (field_v if fy else turned_v).at[pl.ds(first, EDGE)],
+            field_v.at[pl.ds(at, EDGE)],
             2,
             (neighbour(m), me),
         ).start()
@@ -288,7 +292,7 @@
                     first = h * LANES + p * 8
                     back_v[first : first + 16, at] = jnp.concatenate(backs[h], axis=0).astype(BF16)
     prod = 0.125 * lax.dot_general(
-        interp, back_v[...], (((1,), (1,)), ((), ())), preferred_element_type=F32
+        interp_v[...].reshape(NCD // 2, WIDE), back_v[...], (((1,), (1,)), ((), ())), preferred_element_type=F32
     )
     for h in range(2):
         send_e[:, h] = prod[:, h * LANES : (h + 1) * LANES].astype(BF16).reshape(NX, 32, LANES)
@@ -324,10 +328,11 @@
     children = child_out.transpose(1, 2, 0).reshape(2, RHS, width, count)
     out = pl.pallas_call(
         kernel,
-        out_shape=jax.ShapeDtypeStruct((cols * width, count), BF16),
+        out_shape=pltpu.VMEM((cols * width, count), BF16),
         in_specs=[pl.BlockSpec(memory_space=pl.ANY)] * 6,
         out_specs=pl.BlockSpec(memory_space=pltpu.VMEM),
         scratch_shapes=[
+            pltpu.VMEM((2, RHS, 32, LANES), BF16),
             pltpu.VMEM((NX, 32, WIDE), BF16),
             pltpu.VMEM((8, WIDE), F32),
             pltpu.VMEM((NT, 2, LANES), F32),

time: 52 us -> 50.1 us (0.963)
  Pallas kernels: 50.4 us -> 49.3 us
  local copies, waits for them, and re-layouts: 1.47 us -> 0.63 us
    pallas_call x1, Pallas kernels: 50.4 us -> 49.3 us  [per_device(): pl.pallas_call(kernel, out_shape=pltpu.VMEM((cols * width, count), BF16),...]
    unnamed x1, local copies, waits for them, and re-layouts: 1.47 us -> 0.63 us
where the time goes in v4:
time: 50.1 us; the launch traced here: 49.9 us
  Pallas kernels  49.3 us (98%)
  local copies, waits for them, and re-layouts  0.63 us (1%)
    pallas_call x1, Pallas kernels, per_device(): pl.pallas_call(kernel, out_shape=pltpu.VMEM((cols * width, count), BF16),...  49.3 us

profile of v4, /device:TPU:1, one launch (start us, length us, event | category | flops | bytes accessed | tf_op | source)
XLA Modules:
  0.0 49.9 jit_solution(10514244070232026879)
XLA Ops:
  0.0 49.3 %shard_map.64 = bf16[256,128]{1,0:T(8,128)(2,1)S(1)} custom-call(bf16[2,4,32,128]{3,2,1,0:T(8,128)(2,1)} %bitcast.13, bf16[8,2,32,2048]{3,2,1,0:T(8,128)(2,1)} %bitcast.10, f32[8,2048]{1,0:T(8,128)} %angle_hbm.1, f32[343,2,128]{2,1,0:T(2,128)} %trans_hbm.1, s32[27,1024]{1,0:T(8,128)} %bitcast.11, s32[27,1024]{1,0:T(8,128)} %bitcast.12), custom_call_target="tpu_custom_call" | custom-call | tf_op jit(solution)/shard_map/pallas_call | solution.py:329
  49.3 0.6 %copy.8 = bf16[128,8,32]{0,2,1:T(8,128)(2,1)} copy(bf16[128,8,32]{0,2,1:T(8,128)(2,1)S(1)} %bitcast.9) | data formatting | bytes 131072

commit v5 on v4

--- a/solution.py
+++ b/solution.py
@@ -15,7 +15,6 @@
 NT = 343
 NX = 8
 NY = 8
-WIDE = NPD // 2
 RHS = 4
 LAYERS = 4
 BLK = 16
@@ -24,7 +23,10 @@
 EDGE = 48
 HALO = GROUP + 8 * EDGE
 HALO_PAD = 512
-NT_SENT = 352
+NT_HALF = 176
+NT_SENT = 2 * NT_HALF
+MINE = BLK // 2
+PAIR = 2 * NY
 NT_PAD = 384
 STEP = 9
 TURNS = [m for m in range(9) if m != 4]
@@ -37,7 +39,7 @@
 def kernel(
     child_hbm, interp_hbm, angle_hbm, trans_hbm, nidx_hbm, ntr_hbm, out_ref,
     child_v, interp_v, angle_v, trans_v, nidx_v, ntr_v,
-    recv_a, cos_v, sin_v, table_out, table_v, send_b, recv_b, field_v, turned_v,
+    send_a, recv_a, cos_v, sin_v, table_out, table_v, send_b, recv_b, field_v, turned_v,
     pick_v, factor_v, send_d, recv_d, parent_v, back_v, send_e, recv_e,
     load_sem, send_sem, recv_sem,
 ):
@@ -50,6 +52,9 @@
     mx = me // 2
     half = me % 2
     my = half * 4 + layer
+    core = zc % 2
+    part = mx % 2
+    lead = mx - part
 
     def device(x, y):
         return ((y % 4) * 16 + zc, x * 2 + y // 4)
@@ -80,15 +85,11 @@
     for m in TURNS:
         pl.semaphore_signal(barrier, inc=1, device_id=(neighbour(m), me), device_id_type=MESH)
 
-    copies = [
-        (child_hbm, child_v),
-        (trans_hbm, trans_v),
-        (nidx_hbm, nidx_v),
-        (ntr_hbm, ntr_v),
-    ]
-    for q in range(LAYERS):
-        at = pl.ds(pl.multiple_of((mx + 7 + q) % NX * 256, 256), 256)
-        to = pl.ds(q * 256, 256)
+    copies = [(child_hbm, child_v), (trans_hbm, trans_v), (nidx_hbm, nidx_v), (ntr_hbm, ntr_v)]
+    for c in range(8):
+        column = (lead + (c + 5 if c < 4 else 16 - c)) % NX
+        at = pl.ds(pl.multiple_of(column * 256, 256), 256)
+        to = pl.ds(c * 256, 256)
         copies.append((angle_hbm.at[:, at], angle_v.at[:, to]))
         copies.append((interp_hbm.at[:, half, :, at], interp_v.at[:, :, to]))
     loads = [pltpu.make_async_copy(src, dst, load_sem.at[i]) for i, (src, dst) in enumerate(copies)]
@@ -96,12 +97,23 @@
         load.start()
 
     loads[0].wait()
-    recv_a[mx] = child_v[:, mx % 4]
+    left = lax.broadcasted_iota(jnp.int32, (32, LANES), 1) < LANES // 2
+
+    def swap_halves(first, second):
+        first, second = first.astype(F32), second.astype(F32)
+        return (
+            jnp.where(left, first, pltpu.roll(second, LANES // 2, 1)).astype(BF16),
+            jnp.where(left, pltpu.roll(first, LANES // 2, 1), second).astype(BF16),
+        )
+
+    for c in range(RHS):
+        send_a[2 * c], send_a[2 * c + 1] = swap_halves(child_v[0, c], child_v[1, c])
+    recv_a[mx] = send_a[mx]
     pl.semaphore_wait(barrier, (NX - 1) + (NY - 1) + len(TURNS))
 
     def send_child(t, carry):
         to = (mx + far_first(t)) % NX
-        send(child_v.at[:, to % 4], recv_a.at[mx], 0, device(to, my)).start()
+        send(send_a.at[to], recv_a.at[mx], 0, device(to, my)).start()
         return carry
 
     lax.fori_loop(0, NX - 1, send_child, 0)
@@ -112,9 +124,9 @@
             [trans_v[:, h, :], jnp.zeros((NT_SENT - NT, LANES), F32)], axis=0
         ).astype(BF16)
     table_v[NT_SENT:NT_PAD, :] = jnp.zeros((NT_PAD - NT_SENT, 2 * LANES), BF16)
-    table_in = table_v.at[pl.ds(0, NT_SENT)]
-    for q in range(LAYERS):
-        loads[4 + 2 * q].wait()
+    table_in = table_v.at[pl.ds(pl.multiple_of(core * NT_HALF, 16), NT_HALF)]
+    for c in range(8):
+        loads[4 + 2 * c].wait()
     cos_v[...] = jnp.cos(angle_v[...])
     sin_v[...] = jnp.sin(angle_v[...])
 
@@ -161,61 +173,78 @@
     new = lax.broadcasted_iota(jnp.int32, (2 * GROUP, GROUP), 0)
     old = lax.broadcasted_iota(jnp.int32, (2 * GROUP, GROUP), 1)
     px = old % 2 + 2 * ((old // 4) % 2)
-    py = (old // 2) % 2 + 2 * ((old // 8) % 2)
-    straight = 16 * py + 4 * px + old // 16
-    turned = GROUP + 16 * px + 4 * py + old // 16
+    py = (old // 2) % 2 + 2 * (old // 32)
+    pz = (old // 8) % 4
+    straight = 16 * py + 4 * px + pz
+    turned = GROUP + 16 * px + 4 * py + pz
     in_order = jnp.where((straight == new) | (turned == new), 1.0, 0.0).astype(BF16)
 
-    for q in range(LAYERS):
-        loads[5 + 2 * q].wait()
+    for c in range(8):
+        loads[5 + 2 * c].wait()
     wait_for(recv_a.at[pl.ds(0, NX - 1)], recv_sem.at[0])
-    send_table = send(table_out, table_in, 5, device((mx + 9 - layer) % NX, my))
-
-    @pl.when(layer != 1)
+    children = lax.dot_general(
+        by_child, recv_a[...].reshape(NCD // 2, LANES), (((1,), (1,)), ((), ())),
+        preferred_element_type=F32,
+    ).astype(BF16)
+    my_part = part * NY + my
+    for turn in (0, 3, 1, 2):
+        q = (layer + turn) % LAYERS
+        for w in range(2):
+            first = (4 * w + q) * 256
+            some = interp_v[:, :, pl.ds(pl.multiple_of(first, 256), 256)]
+            prod = jnp.dot(children, some.reshape(NCD // 2, 256), preferred_element_type=F32)
+            for i in range(2):
+                at = pl.ds(pl.multiple_of(first + i * LANES, LANES), LANES)
+                total_re = jnp.zeros((MINE, LANES), F32)
+                total_im = jnp.zeros((MINE, LANES), F32)
+                for o in range(8):
+                    re = prod[o * 16 : o * 16 + 8, i * LANES : (i + 1) * LANES]
+                    im = prod[o * 16 + 8 : o * 16 + 16, i * LANES : (i + 1) * LANES]
+                    cosine = cos_v[pl.ds(o, 1), at]
+                    sine = sin_v[pl.ds(o, 1), at]
+                    total_re = total_re + (re * cosine - im * sine)
+                    total_im = total_im + (re * sine + im * cosine)
+                to = i * 4 + q
+                send_b[w * NY + to] = jnp.concatenate([total_re, total_im], axis=0).astype(BF16)
+
+                @pl.when(w * NY + to != my_part)
+                def _(w=w, to=to):
+                    send(
+                        send_b.at[w * NY + to], recv_b.at[my_part], 1, device(lead + w, to)
+                    ).start()
+
+    recv_b[my_part] = send_b[my_part]
+
+    even = (mx + layer) % 2
+    send_table = send(
+        table_out.at[pl.ds(pl.multiple_of(core * NT_HALF, 16), NT_HALF)],
+        table_in,
+        5,
+        device((mx + even * (3 - layer) + (1 - even) * (5 + layer)) % NX, my),
+    )
+
+    @pl.when(layer != 3)
     def _():
         send_table.start()
 
-    @pl.when(layer == 1)
+    @pl.when(layer == 3)
     def _():
-        pltpu.make_async_copy(table_out, table_in, recv_sem.at[5]).start()
-
-    children = jnp.concatenate(
+        pltpu.make_async_copy(
+            table_out.at[pl.ds(pl.multiple_of(core * NT_HALF, 16), NT_HALF)], table_in, recv_sem.at[5]
+        ).start()
+
+    wait_for(recv_b.at[pl.ds(0, PAIR - 1)], recv_sem.at[1])
+    whole = []
+    for w in range(2):
+        early = recv_b[w * NY : w * NY + 4].astype(F32)
+        whole.append(early + recv_b[w * NY + 4 : w * NY + 8].astype(F32))
+    whole = jnp.concatenate(
         [
-            lax.dot_general(
-                by_child, recv_a[:, h].reshape(NCD // 2, LANES), (((1,), (1,)), ((), ())),
-                preferred_element_type=F32,
-            ).astype(BF16)
+            jnp.concatenate([total[:, h * 8 : h * 8 + 8] for total in whole], axis=0).reshape(GROUP, LANES)
             for h in range(2)
         ],
-        axis=0,
-    )
-    for turn in (0, 3, 1, 2):
-        q = (layer + turn) % LAYERS
-        some = interp_v[:, :, pl.ds(pl.multiple_of(q * 256, 256), 256)]
-        prod = jnp.dot(children, some.reshape(NCD // 2, 256), preferred_element_type=F32)
-        for i in range(2):
-            at = pl.ds(pl.multiple_of(q * 256 + i * LANES, LANES), LANES)
-            total_re = jnp.zeros((BLK, LANES), F32)
-            total_im = jnp.zeros((BLK, LANES), F32)
-            for o in range(8):
-                re = prod[o * BLK : (o + 1) * BLK, i * LANES : (i + 1) * LANES]
-                im = prod[LANES + o * BLK : LANES + (o + 1) * BLK, i * LANES : (i + 1) * LANES]
-                cosine = cos_v[pl.ds(o, 1), at]
-                sine = sin_v[pl.ds(o, 1), at]
-                total_re = total_re + (re * cosine - im * sine)
-                total_im = total_im + (re * sine + im * cosine)
-            send_b[i * 4 + q, 0] = total_re.astype(BF16)
-            send_b[i * 4 + q, 1] = total_im.astype(BF16)
-
-            @pl.when(i * 4 + q != my)
-            def _(to=i * 4 + q):
-                send(send_b.at[to], recv_b.at[my], 1, device(mx, to)).start()
-
-    recv_b[my] = send_b[my]
-
-    wait_for(recv_b.at[pl.ds(0, NY - 1)], recv_sem.at[1])
-    whole = (recv_b[0:4].astype(F32) + recv_b[4:8].astype(F32)).astype(BF16)
-    whole = jnp.concatenate([whole[:, h].reshape(GROUP, LANES) for h in range(2)], axis=1)
+        axis=1,
+    ).astype(BF16)
     ordered = jnp.dot(in_order, whole, preferred_element_type=F32).astype(BF16)
     field_v[0:GROUP, :] = ordered[0:GROUP]
     turned_v[...] = ordered[GROUP : 2 * GROUP]
@@ -235,6 +264,9 @@
         ).start()
 
     wait_for(table_in, recv_sem.at[5])
+    swap_table = send(table_in, table_in, 6, (box + 1 - 2 * core, me))
+    swap_table.start()
+    swap_table.wait_recv()
     factor_no = lax.broadcasted_iota(jnp.int32, (GROUP, NT_PAD), 1).astype(F32)
     for s in range(0, NBR, STEP):
         chosen = jnp.concatenate(
@@ -263,39 +295,45 @@
             t_im = factor_v[at : at + GROUP, LANES : 2 * LANES]
             sum_re = sum_re + (re * t_re - im * t_im)
             sum_im = sum_im + (re * t_im + im * t_re)
-    for h, total in enumerate((sum_re, sum_im)):
-        send_d[:, h] = total.astype(BF16).reshape(LAYERS, BLK, LANES)
+    for q in range(LAYERS):
+        for w in range(2):
+            rows = slice(q * BLK + w * MINE, q * BLK + (w + 1) * MINE)
+            send_d[2 * q + w] = jnp.concatenate([sum_re[rows], sum_im[rows]], axis=0).astype(BF16)
 
     def send_sum(t, carry):
-        to = (my + far_first(t)) % NY
-        send(send_d.at[to % 4], recv_d.at[my], 3, device(mx, to)).start()
+        to = (my + far_first(t // 2)) % NY
+        w = (part + 1 - t % 2) % 2
+        send(
+            send_d.at[2 * (to % 4) + w], recv_d.at[my_part], 3, device(lead + w, to)
+        ).start()
         return carry
 
-    lax.fori_loop(0, NY - 1, send_sum, 0)
-    recv_d[my] = send_d[layer]
-
-    wait_for(recv_d.at[pl.ds(0, NY - 1)], recv_sem.at[3])
+    lax.fori_loop(0, PAIR - 1, send_sum, 0)
+    recv_d[my_part] = send_d[2 * layer + part]
+
+    wait_for(recv_d.at[pl.ds(0, PAIR - 1)], recv_sem.at[3])
     parent_v[...] = recv_d[...].astype(F32)
-    for i in range(2):
-        for q in range(LAYERS):
-            at = slice(q * 256 + i * LANES, q * 256 + (i + 1) * LANES)
+    for c in range(8):
+        for i in range(2):
+            slot = (c // 4) * NY + i * 4 + c % 4
+            at = slice(c * 256 + i * LANES, c * 256 + (i + 1) * LANES)
             cosine = cos_v[:, at]
             sine = sin_v[:, at]
-            for p in range(0, BLK, 2):
+            for p in range(0, MINE, 2):
                 backs = [[], []]
                 for r in range(p, p + 2):
-                    re = parent_v[i * 4 + q, 0, r : r + 1, :]
-                    im = parent_v[i * 4 + q, 1, r : r + 1, :]
+                    re = parent_v[slot, r : r + 1, :]
+                    im = parent_v[slot, MINE + r : MINE + r + 1, :]
                     backs[0].append(re * cosine + im * sine)
                     backs[1].append(im * cosine - re * sine)
                 for h in range(2):
-                    first = h * LANES + p * 8
+                    first = h * 64 + p * 8
                     back_v[first : first + 16, at] = jnp.concatenate(backs[h], axis=0).astype(BF16)
     prod = 0.125 * lax.dot_general(
-        interp_v[...].reshape(NCD // 2, WIDE), back_v[...], (((1,), (1,)), ((), ())), preferred_element_type=F32
+        interp_v[...].reshape(NCD // 2, NPD), back_v[...], (((1,), (1,)), ((), ())),
+        preferred_element_type=F32,
     )
-    for h in range(2):
-        send_e[:, h] = prod[:, h * LANES : (h + 1) * LANES].astype(BF16).reshape(NX, 32, LANES)
+    send_e[...] = prod.astype(BF16).reshape(NX, 32, LANES)
 
     def send_result(t, carry):
         to = (mx + far_first(t)) % NX
@@ -305,22 +343,22 @@
     lax.fori_loop(0, NX - 1, send_result, 0)
     recv_e[mx] = send_e[mx]
     wait_for(recv_e.at[pl.ds(0, NX - 1)], recv_sem.at[4])
-    for h in range(2):
-        for c in range(RHS):
-            first = h * LANES + c * 32
-            out_ref[first : first + 32, :] = (
-                recv_e[c, h].astype(F32) + recv_e[c + 4, h].astype(F32)
-            ).astype(BF16)
+    for c in range(RHS):
+        real, imag = swap_halves(recv_e[2 * c], recv_e[2 * c + 1])
+        out_ref[c * 32 : (c + 1) * 32, :] = real
+        out_ref[LANES + c * 32 : LANES + (c + 1) * 32, :] = imag
 
     wait_for(recv_a.at[pl.ds(0, NX - 1)], send_sem.at[0])
-    wait_for(send_b.at[pl.ds(0, NY - 1)], send_sem.at[1])
+    wait_for(send_b.at[pl.ds(0, PAIR - 1)], send_sem.at[1])
     wait_for(field_v.at[pl.ds(0, 8 * EDGE)], send_sem.at[2])
-    wait_for(recv_d.at[pl.ds(0, NY - 1)], send_sem.at[3])
+    wait_for(recv_d.at[pl.ds(0, PAIR - 1)], send_sem.at[3])
     wait_for(send_e.at[pl.ds(0, NX - 1)], send_sem.at[4])
 
-    @pl.when(layer != 1)
+    swap_table.wait_send()
+
+    @pl.when(layer != 3)
     def _():
-        wait_for(table_out, send_sem.at[5])
+        wait_for(table_in, send_sem.at[5])
 
 
 def per_device(child_out, interp, shift_angle, translators, nbr_index, nbr_trans):
@@ -333,31 +371,32 @@
         out_specs=pl.BlockSpec(memory_space=pltpu.VMEM),
         scratch_shapes=[
             pltpu.VMEM((2, RHS, 32, LANES), BF16),
-            pltpu.VMEM((NX, 32, WIDE), BF16),
-            pltpu.VMEM((8, WIDE), F32),
+            pltpu.VMEM((NX, 32, NPD), BF16),
+            pltpu.VMEM((8, NPD), F32),
             pltpu.VMEM((NT, 2, LANES), F32),
             pltpu.VMEM((NBR, 1024), jnp.int32),
             pltpu.VMEM((NBR, 1024), jnp.int32),
-            pltpu.VMEM((NX, 2, 32, LANES), BF16),
-            pltpu.VMEM((8, WIDE), F32),
-            pltpu.VMEM((8, WIDE), F32),
+            pltpu.VMEM((NX, 32, LANES), BF16),
+            pltpu.VMEM((NX, 32, LANES), BF16),
+            pltpu.VMEM((8, NPD), F32),
+            pltpu.VMEM((8, NPD), F32),
             pltpu.VMEM((NT_SENT, 2 * LANES), BF16),
             pltpu.VMEM((NT_PAD, 2 * LANES), BF16),
-            pltpu.VMEM((NY, 2, BLK, LANES), BF16),
-            pltpu.VMEM((NY, 2, BLK, LANES), BF16),
+            pltpu.VMEM((PAIR, 16, LANES), BF16),
+            pltpu.VMEM((PAIR, 16, LANES), BF16),
             pltpu.VMEM((HALO_PAD, 2 * LANES), BF16),
             pltpu.VMEM((GROUP, 2 * LANES), BF16),
             pltpu.VMEM((NBR * GROUP, HALO_PAD), BF16),
             pltpu.VMEM((NBR * GROUP, 2 * LANES), F32),
-            pltpu.VMEM((LAYERS, 2, BLK, LANES), BF16),
-            pltpu.VMEM((NY, 2, BLK, LANES), BF16),
-            pltpu.VMEM((NY, 2, BLK, LANES), F32),
-            pltpu.VMEM((2 * LANES, WIDE), BF16),
-            pltpu.VMEM((NX, 2, 32, LANES), BF16),
-            pltpu.VMEM((NX, 2, 32, LANES), BF16),
-            pltpu.SemaphoreType.DMA((12,)),
-            pltpu.SemaphoreType.DMA((6,)),
-            pltpu.SemaphoreType.DMA((6,)),
+            pltpu.VMEM((2 * LAYERS, 16, LANES), BF16),
+            pltpu.VMEM((PAIR, 16, LANES), BF16),
+            pltpu.VMEM((PAIR, 16, LANES), F32),
+            pltpu.VMEM((LANES, NPD), BF16),
+            pltpu.VMEM((NX, 32, LANES), BF16),
+            pltpu.VMEM((NX, 32, LANES), BF16),
+            pltpu.SemaphoreType.DMA((20,)),
+            pltpu.SemaphoreType.DMA((7,)),
+            pltpu.SemaphoreType.DMA((7,)),
         ],
         compiler_params=pltpu.CompilerParams(
             collective_id=0, has_side_effects=True, vmem_limit_bytes=60 * 1024 * 1024

time: 50.1 us -> 49.4 us (0.986)
  Pallas kernels: 49.3 us -> 48.6 us
    pallas_call x1, Pallas kernels: 49.3 us -> 48.6 us  [per_device(): pl.pallas_call(kernel, out_shape=pltpu.VMEM((cols * width, count), BF16),...]
where the time goes in v5:
time: 49.4 us; the launch traced here: 49.3 us
  Pallas kernels  48.6 us (98%)
  local copies, waits for them, and re-layouts  0.63 us (1%)
    pallas_call x1, Pallas kernels, per_device(): pl.pallas_call(kernel, out_shape=pltpu.VMEM((cols * width, count), BF16),...  48.6 us

profile of v5, /device:TPU:1, one launch (start us, length us, event | category | flops | bytes accessed | tf_op | source)
XLA Modules:
  0.0 49.3 jit_solution(17287136977238632696)
XLA Ops:
  0.0 48.6 %shard_map.64 = bf16[256,128]{1,0:T(8,128)(2,1)S(1)} custom-call(bf16[2,4,32,128]{3,2,1,0:T(8,128)(2,1)} %bitcast.13, bf16[8,2,32,2048]{3,2,1,0:T(8,128)(2,1)} %bitcast.10, f32[8,2048]{1,0:T(8,128)} %angle_hbm.1, f32[343,2,128]{2,1,0:T(2,128)} %trans_hbm.1, s32[27,1024]{1,0:T(8,128)} %bitcast.11, s32[27,1024]{1,0:T(8,128)} %bitcast.12), custom_call_target="tpu_custom_call" | custom-call | tf_op jit(solution)/shard_map/pallas_call | solution.py:367
  48.6 0.6 %copy.8 = bf16[128,8,32]{0,2,1:T(8,128)(2,1)} copy(bf16[128,8,32]{0,2,1:T(8,128)(2,1)S(1)} %bitcast.9) | data formatting | bytes 131072

commit v6 on v5

--- a/solution.py
+++ b/solution.py
@@ -40,8 +40,8 @@
     child_hbm, interp_hbm, angle_hbm, trans_hbm, nidx_hbm, ntr_hbm, out_ref,
     child_v, interp_v, angle_v, trans_v, nidx_v, ntr_v,
     send_a, recv_a, cos_v, sin_v, table_out, table_v, send_b, recv_b, field_v, turned_v,
-    pick_v, factor_v, send_d, recv_d, parent_v, back_v, send_e, recv_e,
-    load_sem, send_sem, recv_sem,
+    pick_v, factor_v, send_d, recv_d, parent_v, back_v, flip_v, send_e, recv_e,
+    load_sem, send_sem, recv_sem, sum_sem,
 ):
     box = lax.axis_index("box")
     me = lax.axis_index("dir")
@@ -181,6 +181,9 @@
 
     for c in range(8):
         loads[5 + 2 * c].wait()
+    for d in range(PAIR):
+        at = slice(d * LANES, (d + 1) * LANES)
+        flip_v[at, :] = interp_v[:, :, at].reshape(NCD // 2, LANES).astype(F32).T.astype(BF16)
     wait_for(recv_a.at[pl.ds(0, NX - 1)], recv_sem.at[0])
     children = lax.dot_general(
         by_child, recv_a[...].reshape(NCD // 2, LANES), (((1,), (1,)), ((), ())),
@@ -300,40 +303,43 @@
             rows = slice(q * BLK + w * MINE, q * BLK + (w + 1) * MINE)
             send_d[2 * q + w] = jnp.concatenate([sum_re[rows], sum_im[rows]], axis=0).astype(BF16)
 
+    def slice_at(t):
+        return (part + 1 - t % 2) % 2, (my + far_first(t // 2)) % NY
+
     def send_sum(t, carry):
-        to = (my + far_first(t // 2)) % NY
-        w = (part + 1 - t % 2) % 2
-        send(
-            send_d.at[2 * (to % 4) + w], recv_d.at[my_part], 3, device(lead + w, to)
+        w, to = slice_at(t)
+        pltpu.make_async_remote_copy(
+            src_ref=send_d.at[2 * (to % 4) + w], dst_ref=recv_d.at[my_part],
+            send_sem=send_sem.at[3], recv_sem=sum_sem.at[my_part],
+            device_id=device(lead + w, to), device_id_type=MESH,
         ).start()
         return carry
 
     lax.fori_loop(0, PAIR - 1, send_sum, 0)
     recv_d[my_part] = send_d[2 * layer + part]
 
-    wait_for(recv_d.at[pl.ds(0, PAIR - 1)], recv_sem.at[3])
-    parent_v[...] = recv_d[...].astype(F32)
-    for c in range(8):
-        for i in range(2):
-            slot = (c // 4) * NY + i * 4 + c % 4
-            at = slice(c * 256 + i * LANES, c * 256 + (i + 1) * LANES)
-            cosine = cos_v[:, at]
-            sine = sin_v[:, at]
-            for p in range(0, MINE, 2):
-                backs = [[], []]
-                for r in range(p, p + 2):
-                    re = parent_v[slot, r : r + 1, :]
-                    im = parent_v[slot, MINE + r : MINE + r + 1, :]
-                    backs[0].append(re * cosine + im * sine)
-                    backs[1].append(im * cosine - re * sine)
-                for h in range(2):
-                    first = h * 64 + p * 8
-                    back_v[first : first + 16, at] = jnp.concatenate(backs[h], axis=0).astype(BF16)
-    prod = 0.125 * lax.dot_general(
-        interp_v[...].reshape(NCD // 2, NPD), back_v[...], (((1,), (1,)), ((), ())),
-        preferred_element_type=F32,
-    )
-    send_e[...] = prod.astype(BF16).reshape(NX, 32, LANES)
+    for t in range(PAIR - 1, -1, -1):
+        w, to = slice_at(t)
+        slot = w * NY + to
+        if t < PAIR - 1:
+            wait_for(recv_d.at[slot], sum_sem.at[slot])
+        parent_v[t] = recv_d[slot].astype(F32)
+        first = (4 * w + to % 4) * 256 + to // 4 * LANES
+        at = pl.ds(pl.multiple_of(first, LANES), LANES)
+        cosine = cos_v[:, at]
+        sine = sin_v[:, at]
+        for p in range(0, MINE, 2):
+            backs = [[], []]
+            for r in range(p, p + 2):
+                re = parent_v[t, r : r + 1, :]
+                im = parent_v[t, MINE + r : MINE + r + 1, :]
+                backs[0].append(re * cosine + im * sine)
+                backs[1].append(im * cosine - re * sine)
+            for h in range(2):
+                rows = slice(h * 64 + p * 8, h * 64 + p * 8 + 16)
+                back_v[rows, at] = jnp.concatenate(backs[h], axis=0).astype(BF16)
+    prod = 0.125 * jnp.dot(back_v[...], flip_v[...], preferred_element_type=F32)
+    send_e[...] = prod.T.astype(BF16).reshape(NX, 32, LANES)
 
     def send_result(t, carry):
         to = (mx + far_first(t)) % NX
@@ -392,11 +398,13 @@
             pltpu.VMEM((PAIR, 16, LANES), BF16),
             pltpu.VMEM((PAIR, 16, LANES), F32),
             pltpu.VMEM((LANES, NPD), BF16),
+            pltpu.VMEM((NPD, NCD // 2), BF16),
             pltpu.VMEM((NX, 32, LANES), BF16),
             pltpu.VMEM((NX, 32, LANES), BF16),
             pltpu.SemaphoreType.DMA((20,)),
             pltpu.SemaphoreType.DMA((7,)),
             pltpu.SemaphoreType.DMA((7,)),
+            pltpu.SemaphoreType.DMA((PAIR,)),
         ],
         compiler_params=pltpu.CompilerParams(
             collective_id=0, has_side_effects=True, vmem_limit_bytes=60 * 1024 * 1024

time: 49.4 us -> 48.9 us (0.990)
  Pallas kernels: 48.6 us -> 48.1 us
    pallas_call x1, Pallas kernels: 48.6 us -> 48.1 us  [per_device(): pl.pallas_call(kernel, out_shape=pltpu.VMEM((cols * width, count), BF16),...]
where the time goes in v6:
time: 48.9 us; the launch traced here: 48.7 us
  Pallas kernels  48.1 us (98%)
  local copies, waits for them, and re-layouts  0.63 us (1%)
    pallas_call x1, Pallas kernels, per_device(): pl.pallas_call(kernel, out_shape=pltpu.VMEM((cols * width, count), BF16),...  48.1 us

profile of v6, /device:TPU:1, one launch (start us, length us, event | category | flops | bytes accessed | tf_op | source)
XLA Modules:
  0.0 48.7 jit_solution(4970906141844109384)
XLA Ops:
  0.0 48.1 %shard_map.64 = bf16[256,128]{1,0:T(8,128)(2,1)S(1)} custom-call(bf16[2,4,32,128]{3,2,1,0:T(8,128)(2,1)} %bitcast.13, bf16[8,2,32,2048]{3,2,1,0:T(8,128)(2,1)} %bitcast.10, f32[8,2048]{1,0:T(8,128)} %angle_hbm.1, f32[343,2,128]{2,1,0:T(2,128)} %trans_hbm.1, s32[27,1024]{1,0:T(8,128)} %bitcast.11, s32[27,1024]{1,0:T(8,128)} %bitcast.12), custom_call_target="tpu_custom_call" | custom-call | tf_op jit(solution)/shard_map/pallas_call | solution.py:373
  48.1 0.6 %copy.8 = bf16[128,8,32]{0,2,1:T(8,128)(2,1)} copy(bf16[128,8,32]{0,2,1:T(8,128)(2,1)S(1)} %bitcast.9) | data formatting | bytes 131072

commit v7 on v6

--- a/solution.py
+++ b/solution.py
@@ -28,7 +28,7 @@
 MINE = BLK // 2
 PAIR = 2 * NY
 NT_PAD = 384
-STEP = 9
+PICKS = NBR * BLK
 TURNS = [m for m in range(9) if m != 4]
 
 
@@ -160,11 +160,15 @@
     source_rows = row.astype(F32).T[0:GROUP, :]
     factor_rows = mine(ntr_v).astype(F32).T[0:GROUP, :]
 
-    slot_no = lax.broadcasted_iota(jnp.int32, (GROUP, HALO_PAD), 1).astype(F32)
-    for n in range(NBR):
-        pick_v[n * GROUP : (n + 1) * GROUP, :] = jnp.where(
-            source_rows[:, n : n + 1] == slot_no, 1.0, 0.0
+    def select(rows, count, q):
+        number = lax.broadcasted_iota(jnp.int32, (BLK, count), 1).astype(F32)
+        mine = rows[q * BLK : (q + 1) * BLK, :]
+        return jnp.concatenate(
+            [jnp.where(mine[:, n : n + 1] == number, 1.0, 0.0) for n in range(NBR)], axis=0
         ).astype(BF16)
+
+    for q in range(LAYERS):
+        pick_v[q * PICKS : (q + 1) * PICKS, :] = select(source_rows, HALO_PAD, q)
     field_v[HALO:HALO_PAD, :] = jnp.zeros((HALO_PAD - HALO, 2 * LANES), BF16)
 
     new = lax.broadcasted_iota(jnp.int32, (LANES, LANES), 0)
@@ -270,52 +274,47 @@
     swap_table = send(table_in, table_in, 6, (box + 1 - 2 * core, me))
     swap_table.start()
     swap_table.wait_recv()
-    factor_no = lax.broadcasted_iota(jnp.int32, (GROUP, NT_PAD), 1).astype(F32)
-    for s in range(0, NBR, STEP):
-        chosen = jnp.concatenate(
-            [
-                jnp.where(factor_rows[:, n : n + 1] == factor_no, 1.0, 0.0).astype(BF16)
-                for n in range(s, s + STEP)
-            ],
-            axis=0,
+    for q in range(LAYERS):
+        factor_v[q * PICKS : (q + 1) * PICKS, :] = jnp.dot(
+            select(factor_rows, NT_PAD, q), table_v[...], preferred_element_type=F32
         )
-        factor_v[s * GROUP : (s + STEP) * GROUP, :] = jnp.dot(
-            chosen, table_v[...], preferred_element_type=F32
+
+    wait_for(field_v.at[pl.ds(GROUP, 8 * EDGE)], recv_sem.at[2])
+    def slice_at(t):
+        return (part + 1 - t % 2) % 2, (my + far_first(t // 2)) % NY
+
+    for turn in (0, 3, 1, 2):
+        q = (layer + turn) % LAYERS
+        picked = jnp.dot(
+            pick_v[pl.ds(pl.multiple_of(q * PICKS, 16), PICKS), :],
+            field_v[...],
+            preferred_element_type=F32,
         )
-
-    wait_for(field_v.at[pl.ds(GROUP, 8 * EDGE)], recv_sem.at[2])
-    sum_re = jnp.zeros((GROUP, LANES), F32)
-    sum_im = jnp.zeros((GROUP, LANES), F32)
-    for s in range(0, NBR, STEP):
-        picked = jnp.dot(
-            pick_v[s * GROUP : (s + STEP) * GROUP, :], field_v[...], preferred_element_type=F32
-        )
-        for n in range(STEP):
-            re = picked[n * GROUP : (n + 1) * GROUP, 0:LANES]
-            im = picked[n * GROUP : (n + 1) * GROUP, LANES : 2 * LANES]
-            at = (s + n) * GROUP
-            t_re = factor_v[at : at + GROUP, 0:LANES]
-            t_im = factor_v[at : at + GROUP, LANES : 2 * LANES]
+        sum_re = jnp.zeros((BLK, LANES), F32)
+        sum_im = jnp.zeros((BLK, LANES), F32)
+        for n in range(NBR):
+            re = picked[n * BLK : (n + 1) * BLK, 0:LANES]
+            im = picked[n * BLK : (n + 1) * BLK, LANES : 2 * LANES]
+            at = pl.ds(pl.multiple_of(q * PICKS + n * BLK, 16), BLK)
+            t_re = factor_v[at, 0:LANES]
+            t_im = factor_v[at, LANES : 2 * LANES]
             sum_re = sum_re + (re * t_re - im * t_im)
             sum_im = sum_im + (re * t_im + im * t_re)
-    for q in range(LAYERS):
         for w in range(2):
-            rows = slice(q * BLK + w * MINE, q * BLK + (w + 1) * MINE)
+            rows = slice(w * MINE, (w + 1) * MINE)
             send_d[2 * q + w] = jnp.concatenate([sum_re[rows], sum_im[rows]], axis=0).astype(BF16)
-
-    def slice_at(t):
-        return (part + 1 - t % 2) % 2, (my + far_first(t // 2)) % NY
-
-    def send_sum(t, carry):
-        w, to = slice_at(t)
-        pltpu.make_async_remote_copy(
-            src_ref=send_d.at[2 * (to % 4) + w], dst_ref=recv_d.at[my_part],
-            send_sem=send_sem.at[3], recv_sem=sum_sem.at[my_part],
-            device_id=device(lead + w, to), device_id_type=MESH,
-        ).start()
-        return carry
-
-    lax.fori_loop(0, PAIR - 1, send_sum, 0)
+        for i in (1, 0):
+            to = (half + i) % 2 * 4 + q
+            for w in range(2):
+
+                @pl.when(w * NY + to != my_part)
+                def _(w=w, to=to, q=q):
+                    pltpu.make_async_remote_copy(
+                        src_ref=send_d.at[2 * q + w], dst_ref=recv_d.at[my_part],
+                        send_sem=send_sem.at[3], recv_sem=sum_sem.at[my_part],
+                        device_id=device(lead + w, to), device_id_type=MESH,
+                    ).start()
+
     recv_d[my_part] = send_d[2 * layer + part]
 
     for t in range(PAIR - 1, -1, -1):

time: 48.9 us -> 49.5 us (1.012)
  Pallas kernels: 48.1 us -> 48.7 us
    pallas_call x1, Pallas kernels: 48.1 us -> 48.7 us  [per_device(): pl.pallas_call(kernel, out_shape=pltpu.VMEM((cols * width, count), BF16),...]
where the time goes in v7:
time: 49.5 us; the launch traced here: 49.3 us
  Pallas kernels  48.7 us (98%)
  local copies, waits for them, and re-layouts  0.63 us (1%)
    pallas_call x1, Pallas kernels, per_device(): pl.pallas_call(kernel, out_shape=pltpu.VMEM((cols * width, count), BF16),...  48.7 us

profile of v7, /device:TPU:1, one launch (start us, length us, event | category | flops | bytes accessed | tf_op | source)
XLA Modules:
  0.0 49.3 jit_solution(13047596568784212460)
XLA Ops:
  0.0 48.7 %shard_map.64 = bf16[256,128]{1,0:T(8,128)(2,1)S(1)} custom-call(bf16[2,4,32,128]{3,2,1,0:T(8,128)(2,1)} %bitcast.13, bf16[8,2,32,2048]{3,2,1,0:T(8,128)(2,1)} %bitcast.10, f32[8,2048]{1,0:T(8,128)} %angle_hbm.1, f32[343,2,128]{2,1,0:T(2,128)} %trans_hbm.1, s32[27,1024]{1,0:T(8,128)} %bitcast.11, s32[27,1024]{1,0:T(8,128)} %bitcast.12), custom_call_target="tpu_custom_call" | custom-call | tf_op jit(solution)/shard_map/pallas_call | solution.py:372
  48.7 0.6 %copy.8 = bf16[128,8,32]{0,2,1:T(8,128)(2,1)} copy(bf16[128,8,32]{0,2,1:T(8,128)(2,1)S(1)} %bitcast.9) | data formatting | bytes 131072

commit v8 on v6

--- a/solution.py
+++ b/solution.py
@@ -318,6 +318,8 @@
     lax.fori_loop(0, PAIR - 1, send_sum, 0)
     recv_d[my_part] = send_d[2 * layer + part]
 
+    prod = jnp.zeros((LANES, NCD // 2), F32)
+    weights = []
     for t in range(PAIR - 1, -1, -1):
         w, to = slice_at(t)
         slot = w * NY + to
@@ -337,9 +339,16 @@
                 backs[1].append(im * cosine - re * sine)
             for h in range(2):
                 rows = slice(h * 64 + p * 8, h * 64 + p * 8 + 16)
-                back_v[rows, at] = jnp.concatenate(backs[h], axis=0).astype(BF16)
-    prod = 0.125 * jnp.dot(back_v[...], flip_v[...], preferred_element_type=F32)
-    send_e[...] = prod.T.astype(BF16).reshape(NX, 32, LANES)
+                back_v[rows, t * LANES : (t + 1) * LANES] = jnp.concatenate(backs[h], axis=0).astype(BF16)
+        weights.insert(0, flip_v[at, :])
+        if t % 2 == 0:
+            prod = prod + jnp.dot(
+                back_v[:, t * LANES : (t + 2) * LANES],
+                jnp.concatenate(weights, axis=0),
+                preferred_element_type=F32,
+            )
+            weights = []
+    send_e[...] = (0.125 * prod).T.astype(BF16).reshape(NX, 32, LANES)
 
     def send_result(t, carry):
         to = (mx + far_first(t)) % NX

time: 48.9 us -> 49 us (level)
  no operation moved by 1% of the time
where the time goes in v8:
time: 49 us; the launch traced here: 48.8 us
  Pallas kernels  48.2 us (98%)
  local copies, waits for them, and re-layouts  0.63 us (1%)
    pallas_call x1, Pallas kernels, per_device(): pl.pallas_call(kernel, out_shape=pltpu.VMEM((cols * width, count), BF16),...  48.2 us

profile of v8, /device:TPU:1, one launch (start us, length us, event | category | flops | bytes accessed | tf_op | source)
XLA Modules:
  0.0 48.8 jit_solution(10673950506671433550)
XLA Ops:
  0.0 48.2 %shard_map.64 = bf16[256,128]{1,0:T(8,128)(2,1)S(1)} custom-call(bf16[2,4,32,128]{3,2,1,0:T(8,128)(2,1)} %bitcast.13, bf16[8,2,32,2048]{3,2,1,0:T(8,128)(2,1)} %bitcast.10, f32[8,2048]{1,0:T(8,128)} %angle_hbm.1, f32[343,2,128]{2,1,0:T(2,128)} %trans_hbm.1, s32[27,1024]{1,0:T(8,128)} %bitcast.11, s32[27,1024]{1,0:T(8,128)} %bitcast.12), custom_call_target="tpu_custom_call" | custom-call | tf_op jit(solution)/shard_map/pallas_call | solution.py:382
  48.2 0.6 %copy.8 = bf16[128,8,32]{0,2,1:T(8,128)(2,1)} copy(bf16[128,8,32]{0,2,1:T(8,128)(2,1)S(1)} %bitcast.9) | data formatting | bytes 131072

commit v9 on v6

--- a/solution.py
+++ b/solution.py
@@ -40,7 +40,7 @@
     child_hbm, interp_hbm, angle_hbm, trans_hbm, nidx_hbm, ntr_hbm, out_ref,
     child_v, interp_v, angle_v, trans_v, nidx_v, ntr_v,
     send_a, recv_a, cos_v, sin_v, table_out, table_v, send_b, recv_b, field_v, turned_v,
-    pick_v, factor_v, send_d, recv_d, parent_v, back_v, flip_v, send_e, recv_e,
+    pick_v, chosen_v, factor_v, send_d, recv_d, parent_v, back_v, flip_v, send_e, recv_e,
     load_sem, send_sem, recv_sem, sum_sem,
 ):
     box = lax.axis_index("box")
@@ -164,6 +164,11 @@
     for n in range(NBR):
         pick_v[n * GROUP : (n + 1) * GROUP, :] = jnp.where(
             source_rows[:, n : n + 1] == slot_no, 1.0, 0.0
+        ).astype(BF16)
+    factor_no = lax.broadcasted_iota(jnp.int32, (GROUP, NT_PAD), 1).astype(F32)
+    for n in range(NBR):
+        chosen_v[n * GROUP : (n + 1) * GROUP, :] = jnp.where(
+            factor_rows[:, n : n + 1] == factor_no, 1.0, 0.0
         ).astype(BF16)
     field_v[HALO:HALO_PAD, :] = jnp.zeros((HALO_PAD - HALO, 2 * LANES), BF16)
 
@@ -270,17 +275,9 @@
     swap_table = send(table_in, table_in, 6, (box + 1 - 2 * core, me))
     swap_table.start()
     swap_table.wait_recv()
-    factor_no = lax.broadcasted_iota(jnp.int32, (GROUP, NT_PAD), 1).astype(F32)
     for s in range(0, NBR, STEP):
-        chosen = jnp.concatenate(
-            [
-                jnp.where(factor_rows[:, n : n + 1] == factor_no, 1.0, 0.0).astype(BF16)
-                for n in range(s, s + STEP)
-            ],
-            axis=0,
-        )
         factor_v[s * GROUP : (s + STEP) * GROUP, :] = jnp.dot(
-            chosen, table_v[...], preferred_element_type=F32
+            chosen_v[s * GROUP : (s + STEP) * GROUP, :], table_v[...], preferred_element_type=F32
         )
 
     wait_for(field_v.at[pl.ds(GROUP, 8 * EDGE)], recv_sem.at[2])
@@ -393,6 +390,7 @@
             pltpu.VMEM((HALO_PAD, 2 * LANES), BF16),
             pltpu.VMEM((GROUP, 2 * LANES), BF16),
             pltpu.VMEM((NBR * GROUP, HALO_PAD), BF16),
+            pltpu.VMEM((NBR * GROUP, NT_PAD), BF16),
             pltpu.VMEM((NBR * GROUP, 2 * LANES), F32),
             pltpu.VMEM((2 * LAYERS, 16, LANES), BF16),
             pltpu.VMEM((PAIR, 16, LANES), BF16),

time: 48.9 us -> 48.9 us (level)
  no operation moved by 1% of the time
where the time goes in v9:
time: 48.9 us; the launch traced here: 48.7 us
  Pallas kernels  48.1 us (98%)
  local copies, waits for them, and re-layouts  0.63 us (1%)
    pallas_call x1, Pallas kernels, per_device(): pl.pallas_call(kernel, out_shape=pltpu.VMEM((cols * width, count), BF16),...  48.1 us

profile of v9, /device:TPU:1, one launch (start us, length us, event | category | flops | bytes accessed | tf_op | source)
XLA Modules:
  0.0 48.7 jit_solution(14870910299038045334)
XLA Ops:
  0.0 48.1 %shard_map.64 = bf16[256,128]{1,0:T(8,128)(2,1)S(1)} custom-call(bf16[2,4,32,128]{3,2,1,0:T(8,128)(2,1)} %bitcast.13, bf16[8,2,32,2048]{3,2,1,0:T(8,128)(2,1)} %bitcast.10, f32[8,2048]{1,0:T(8,128)} %angle_hbm.1, f32[343,2,128]{2,1,0:T(2,128)} %trans_hbm.1, s32[27,1024]{1,0:T(8,128)} %bitcast.11, s32[27,1024]{1,0:T(8,128)} %bitcast.12), custom_call_target="tpu_custom_call" | custom-call | tf_op jit(solution)/shard_map/pallas_call | solution.py:370
  48.1 0.6 %copy.8 = bf16[128,8,32]{0,2,1:T(8,128)(2,1)} copy(bf16[128,8,32]{0,2,1:T(8,128)(2,1)S(1)} %bitcast.9) | data formatting | bytes 131072
